TPU v7x, 256 devices: a whole 4x4x8 slice. The times are simulated.
256 devices in a mesh: row: 8 (over x, core), col: 32 (over y, z).
Axes of the slice: x: 4, y: 4, z: 8, core: 2. Of those that a mesh axis runs over, the one named last changes fastest.
Arguments:
- queries: float32 [32, 131072], P(None, ('row', 'col'))
- block_spots: int32 [8, 32, 256], P('row', 'col'), may hold values from 0 to 4095, as said below
- live_blocks: int32 [8, 32], P('row', 'col'), may hold values from 1 to 256, as said below
- neighbor_cols: int32 [8, 32, 256, 16, 128], P('row', 'col'), may hold values from 0 to 127
- neighbor_sims: bfloat16 [8, 32, 256, 16, 128], P('row', 'col'), may hold values from 0.099609375 to 1
Outputs:
- solution: float32 [32, 131072], P(None, ('row', 'col'))
- residual: float32 [32, 131072], P(None, ('row', 'col'))
Inputs may be any that keep to these rules, and one draw needn't show every extreme that they name: `block_spots`: within each index of the first two dimensions the 256 spots are distinct. `live_blocks`: some index of the array holds exactly 256.
All inputs are finite; a program needn't handle non-finite values.
Results may differ from a plain program's by a relative error of at most 0.01.
Values may be sent and summed in bfloat16 or wider, within the bound.
A program may use at most 128 MiB of HBM per device.

v0:
```python
import jax
import jax.numpy as jnp
from jax import lax
from jax.sharding import PartitionSpec as P

ITERS = 2


graph_weight = 0.95


def fill_blocks(neighbor_idx, neighbor_val):
    lane_ids = jnp.arange(128, dtype=jnp.int32)
    running = jnp.zeros((neighbor_idx.shape[0], 128, 128), jnp.float32)
    for column_slot in range(neighbor_idx.shape[1]):
        matched = neighbor_idx[:, column_slot, :, None] == lane_ids
        running = running + jnp.where(
            matched, neighbor_val[:, column_slot, :, None].astype(jnp.float32), jnp.float32(0.0)
        )
    return running.astype(jnp.bfloat16)


def fill_group(group_pair):
    return fill_blocks(group_pair[0], group_pair[1])


def build_blocks(index_table, value_table):
    slot_count = index_table.shape[0]
    index_groups = index_table.reshape(slot_count // 16, 16, index_table.shape[1], 128)
    value_groups = value_table.reshape(slot_count // 16, 16, value_table.shape[1], 128)
    return lax.map(fill_group, (index_groups, value_groups)).reshape(slot_count, 128, 128)


def spd_solve(matrix, right_side):
    factor = jnp.linalg.cholesky(matrix)
    partial_value = lax.linalg.triangular_solve(factor, right_side, left_side=True, lower=True)
    return lax.linalg.triangular_solve(
        factor, partial_value, left_side=True, lower=True, transpose_a=True
    )


def gram_matrix(first_rows, second_rows):
    return lax.dot_general(
        first_rows, second_rows, (((1,), (1,)), ((), ())), precision=lax.Precision.HIGHEST
    )


def symmetric(square):
    return 0.5 * (square + square.T)


def block_products(blocks, spot_list, slot_start, slot_stop, col_dirs, row_dirs):
    query_rows = col_dirs.shape[0]
    row_blocks = row_dirs.shape[1]
    col_blocks = col_dirs.shape[1]
    row_lanes = jnp.arange(row_blocks, dtype=jnp.int32)
    col_lanes = jnp.arange(col_blocks, dtype=jnp.int32)

    def group_turn(turn_index, totals):
        row_total, col_total = totals
        first_slot = turn_index * 16
        group_blocks = lax.dynamic_slice_in_dim(blocks, first_slot, 16, 0)
        group_spots = lax.dynamic_slice_in_dim(spot_list, first_slot, 16, 0)
        slot_ids = first_slot + jnp.arange(16, dtype=jnp.int32)
        active = ((slot_ids >= slot_start) & (slot_ids < slot_stop)).astype(jnp.float32)
        block_row = group_spots // col_blocks
        block_col = group_spots % col_blocks
        col_vecs = jnp.take(col_dirs, block_col, axis=1)
        row_vecs = jnp.take(row_dirs, block_row, axis=1)
        forward = jnp.einsum(
            "sij,msj->msi", group_blocks, col_vecs, preferred_element_type=jnp.float32
        )
        backward = jnp.einsum(
            "sij,msi->msj", group_blocks, row_vecs, preferred_element_type=jnp.float32
        )
        row_select = (block_row[:, None] == row_lanes).astype(jnp.float32) * active[:, None]
        col_select = (block_col[:, None] == col_lanes).astype(jnp.float32) * active[:, None]
        row_total = row_total + jnp.einsum(
            "sb,msi->mbi", row_select, forward, precision=lax.Precision.HIGHEST
        )
        col_total = col_total + jnp.einsum(
            "sb,msi->mbi", col_select, backward, precision=lax.Precision.HIGHEST
        )
        return (row_total, col_total)

    row_zero = jnp.zeros((query_rows, row_blocks, 128), jnp.float32)
    col_zero = jnp.zeros((query_rows, col_blocks, 128), jnp.float32)
    return lax.fori_loop(slot_start // 16, (slot_stop + 15) // 16, group_turn, (row_zero, col_zero))


def body(queries, block_spots, live_blocks, neighbor_cols, neighbor_sims):
    row_count = lax.axis_size("row")
    col_count = lax.axis_size("col")
    seg_len = queries.shape[1]
    per_seg = seg_len // 128
    row_blocks = row_count * per_seg
    col_blocks = col_count * per_seg
    spot_list = block_spots[0, 0]
    live_count = live_blocks[0, 0]
    index_table = neighbor_cols[0, 0]
    value_table = neighbor_sims[0, 0]
    blocks = build_blocks(index_table, value_table)

    def partial_sums(col_dirs, row_dirs):
        query_rows = col_dirs.shape[0]
        row_total, col_total = block_products(
            blocks, spot_list, jnp.int32(0), live_count, col_dirs, row_dirs
        )
        row_sum = lax.psum_scatter(
            row_total.reshape(query_rows, row_blocks * 128), "row", scatter_dimension=1, tiled=True
        )
        col_sum = lax.psum_scatter(
            col_total.reshape(query_rows, col_blocks * 128), "col", scatter_dimension=1, tiled=True
        )
        return 0.5 * (row_sum + col_sum)

    unit_cols = jnp.ones((1, col_blocks, 128), jnp.bfloat16)
    unit_rows = jnp.ones((1, row_blocks, 128), jnp.bfloat16)
    degree = 1.0 + partial_sums(unit_cols, unit_rows)
    scaling = 1.0 / jnp.sqrt(degree)
    solution = jnp.zeros_like(queries)
    residual = queries
    direction = queries

    def residual_gram(current):
        return symmetric(lax.psum(gram_matrix(current, current), ("row", "col")))

    res_gram = residual_gram(residual)
    for sweep_index in range(ITERS):
        scaled = (scaling * direction).astype(jnp.bfloat16)
        operator_query_rows = scaled.shape[0]
        operator_col_dirs = lax.all_gather(scaled, "col", axis=1, tiled=True).reshape(
            operator_query_rows, col_blocks, 128
        )
        operator_row_dirs = lax.all_gather(scaled, "row", axis=1, tiled=True).reshape(
            operator_query_rows, row_blocks, 128
        )
        applied = direction - graph_weight * scaling * partial_sums(
            operator_col_dirs, operator_row_dirs
        )
        curvature = symmetric(lax.psum(gram_matrix(direction, applied), ("row", "col")))
        weights = spd_solve(curvature, res_gram)
        solution = solution + jnp.dot(weights.T, direction, precision=lax.Precision.HIGHEST)
        residual = residual - jnp.dot(weights.T, applied, precision=lax.Precision.HIGHEST)
        if sweep_index + 1 < ITERS:
            new_gram = residual_gram(residual)
            mixing = spd_solve(res_gram, new_gram)
            direction = residual + jnp.dot(mixing.T, direction, precision=lax.Precision.HIGHEST)
            res_gram = new_gram
    return (solution, residual)


def solution(mesh):
    placed = (
        P(None, ("row", "col")),
        P("row", "col", None),
        P("row", "col"),
        P("row", "col", None, None, None),
        P("row", "col", None, None, None),
    )
    return jax.shard_map(
        body,
        mesh=mesh,
        in_specs=placed,
        out_specs=(P(None, ("row", "col")), P(None, ("row", "col"))),
        check_vma=False,
    )
```

profile of v0, /device:TPU:1, one launch (start us, length us, event | category | flops | bytes accessed | tf_op | source)
XLA Modules:
  0.0 1814.3 jit_solution(16293699807531779206)
XLA Ops:
  7.9 190.7 %while.55 = (s32[]{:T(128)}, bf16[16,16,128,128]{3,2,1,0:T(8,128)(2,1)}, s32[16,16,16,128]{3,2,1,0:T(8,128)}, bf16[16,16,16,128]{3,2,1,0:T(8,128)(2,1)}, s32[]{:T(128)}) while((s32[]{:T(128)}, bf16[16,16,128,128]{3,2,1,0:T(8,128)(2,1)}, s32[16,16,16,128]{3,2,1,0:T(8,128)}, bf16[16,16,16,128]{3,2,1,0:T(8,128)(2,1)}, s32[]{:T(128)}) %tuple.198), condition=%wide.region_1.2_spmd, body=%wide.region_0.1_spmd.sunk | while | flops 12615682 | bytes 2032197 | solution.py:31
  9.8 10.0 fusion.198
  21.7 10.0 fusion.198
  33.6 10.0 fusion.198
  45.5 10.0 fusion.198
  57.5 10.0 fusion.198
  69.4 10.0 fusion.198
  93.2 10.0 fusion.198
  105.1 10.0 fusion.198
  117.1 10.0 fusion.198
  129.0 10.0 fusion.198
  140.9 10.0 fusion.198
  152.8 10.0 fusion.198
  164.7 10.0 fusion.198
  176.6 10.0 fusion.198
  188.6 10.0 fusion.198
  198.6 27.4 %while.56 = (s32[]{:T(128)}, f32[1,32,128]{2,1,0:T(8,128)S(1)}, f32[1,128,128]{1,2,0:T(8,128)S(1)}, s32[]{:T(128)}, s32[256]{0:T(256)S(1)}, /*index=5*/bf16[256,...) while((s32[]{:T(128)}, f32[1,32,128]{2,1,0:T(8,128)S(1)}, ...), condition=%wide.region_3.4_spmd.clone, body=%wide.region_2.3_spmd.clone.sunk | while | flops 5013174 | bytes 1336699 | solution.py:88
  233.2 88.5 %reduce-scatter.19.cloned.1.call-done = f32[512,1]{1,0:T(8,128)} async-done(((f32[4096,1]{1,0:T(8,128)}), f32[512,1]{1,0:T(8,128)}) %reduce-scatter.19.cloned.1.call-update) | async-done | bytes 2064
  322.7 229.1 %reduce-scatter.21.cloned.1.call-done = f32[512,1]{1,0:T(8,128)} async-done(((f32[16384,1]{1,0:T(8,128)}), f32[512,1]{1,0:T(8,128)}) %reduce-scatter.21.cloned.1.call-update) | async-done | bytes 2064
  553.6 17.9 all_gather.13
  571.5 53.2 %all-gather.3.cloned.1.call-done = bf16[32,16384]{1,0:T(8,128)(2,1)} async-done(((bf16[32,512]{1,0:T(8,128)(2,1)}), bf16[32,16384]{1,0:T(8,128)(2,1)}) %all-gather.3.cloned.1.call-update) | async-done | bytes 1048592 | tf_op jit(solution)/shard_map/all_gather | solution.py:132
  627.4 55.1 %while.57 = (s32[]{:T(128)}, f32[32,32,128]{2,1,0:T(8,128)S(1)}, f32[32,128,128]{1,2,0:T(8,128)S(1)}, s32[]{:T(128)}, s32[256]{0:T(256)S(1)}, /*index=5*/bf16[32...) while((s32[]{:T(128)}, f32[32,32,128]{2,1,0:T(8,128)S(1)}, ...), condition=%wide.region_7.10_spmd.clone, body=%wide.region_6.9_spmd.clone.sunk | while | flops 160177840 | bytes 8136063 | solution.py:88
  690.1 146.9 %reduce-scatter.11.cloned.1.call-done = f32[32,512]{1,0:T(8,128)} async-done(((f32[32,4096]{1,0:T(8,128)}), f32[32,512]{1,0:T(8,128)}) %reduce-scatter.11.cloned.1.call-update) | async-done | bytes 65552 | tf_op jit(solution)/shard_map/reduce_scatter | solution.py:109
  837.0 215.9 %reduce-scatter.13.cloned.1.call-done = f32[32,512]{1,0:T(8,128)} async-done(((f32[32,16384]{1,0:T(8,128)}), f32[32,512]{1,0:T(8,128)}) %reduce-scatter.13.cloned.1.call-update) | async-done | bytes 65552 | tf_op jit(solution)/shard_map/reduce_scatter | solution.py:112
  1053.9 80.0 %all-reduce = (f32[32,32]{1,0:T(8,128)S(1)}, f32[32,32]{1,0:T(8,128)S(1)}) all-reduce(f32[32,32]{1,0:T(8,128)S(1)} %fusion.138, f32[32,32]{1,0:T(8,128)S(1)} %convolution_bitcast_fusion.8), channel_id=1, replica_groups=mesh['row'=8,'col'=32] {'row','col'}, use_global_device_ids=true, to_apply=%region_13.17 | all-reduce | flops 2048 | bytes 16384 | tf_op jit(solution)/shard_map/psum | solution.py:126
  1149.4 73.7 %psum.30 = f32[32,32]{1,0:T(8,128)S(1)} all-reduce(f32[32,32]{1,0:T(8,128)S(1)} %fusion.140), channel_id=1, replica_groups=mesh['row'=8,'col'=32] {'row','col'}, use_global_device_ids=true, to_apply=%region_14.20 | all-reduce | flops 1024 | bytes 8192 | tf_op jit(solution)/shard_map/psum | solution.py:126
  1224.5 13.6 all_gather.15
  1238.1 49.8 %all-gather.5.cloned.1.call-done = bf16[32,16384]{1,0:T(8,128)(2,1)} async-done(((bf16[32,512]{1,0:T(8,128)(2,1)}), bf16[32,16384]{1,0:T(8,128)(2,1)}) %all-gather.5.cloned.1.call-update) | async-done | bytes 1048592 | tf_op jit(solution)/shard_map/all_gather | solution.py:132
  1290.6 55.4 %while.58 = (s32[]{:T(128)}, f32[32,32,128]{2,1,0:T(8,128)S(1)}, f32[32,128,128]{1,2,0:T(8,128)S(1)}, s32[]{:T(128)}, s32[256]{0:T(256)S(1)}, /*index=5*/bf16[32...) while((s32[]{:T(128)}, f32[32,32,128]{2,1,0:T(8,128)S(1)}, ...), condition=%wide.region_16.22_spmd.clone, body=%wide.region_15.21_spmd.clone.sunk | while | flops 160177840 | bytes 8136063 | solution.py:88
  1353.4 147.0 %reduce-scatter.15.cloned.1.call-done = f32[32,512]{1,0:T(8,128)} async-done(((f32[32,4096]{1,0:T(8,128)}), f32[32,512]{1,0:T(8,128)}) %reduce-scatter.15.cloned.1.call-update) | async-done | bytes 65552 | tf_op jit(solution)/shard_map/reduce_scatter | solution.py:109
  1500.4 216.2 %reduce-scatter.17.cloned.1.call-done = f32[32,512]{1,0:T(8,128)} async-done(((f32[32,16384]{1,0:T(8,128)}), f32[32,512]{1,0:T(8,128)}) %reduce-scatter.17.cloned.1.call-update) | async-done | bytes 65552 | tf_op jit(solution)/shard_map/reduce_scatter | solution.py:112
  1717.6 79.9 %psum.31 = f32[32,32]{1,0:T(8,128)S(1)} all-reduce(f32[32,32]{1,0:T(8,128)S(1)} %fusion.111), channel_id=1, replica_groups=mesh['row'=8,'col'=32] {'row','col'}, use_global_device_ids=true, to_apply=%region_19.25 | all-reduce | flops 1024 | bytes 8192 | tf_op jit(solution)/shard_map/psum | solution.py:141
  (383 shorter events, 235.3 us)
Async XLA Ops:
  7.2 314.5 %reduce-scatter.19.cloned.1.call-start = ((), (), s32[]{:S(2)}) async-start(), calls=%async_computation.12 | async-start | bytes 2359296
  7.9 190.7 %copy-start.1 = (s32[1,1,256]{2,1,0:T(1,128)S(1)}, s32[1,1,256]{2,1,0:T(1,128)}, u32[]{:S(2)}) copy-start(s32[1,1,256]{2,1,0:T(1,128)} %param.23) | copy-start | bytes 3076
  228.0 323.8 %reduce-scatter.21.cloned.1.call-start = ((), (), s32[]{:S(2)}) async-start(), calls=%async_computation.13 | async-start | bytes 8650752
  233.1 319.8 %copy-start = (f32[32,512]{1,0:T(8,128)S(1)}, f32[32,512]{1,0:T(8,128)}, u32[]{:S(2)}) copy-start(f32[32,512]{1,0:T(8,128)} %param.22) | copy-start | bytes 196612
  233.1 391.6 %all-gather.3.cloned.1.call-start = ((), (), s32[]{:S(2)}) async-start(), calls=%async_computation.6 | async-start | bytes 1081344 | tf_op jit(solution)/shard_map/all_gather | solution.py:132
  553.6 283.4 %reduce-scatter.11.cloned.1.call-start = ((), (), s32[]{:S(2)}) async-start(), calls=%async_computation.7 | async-start | bytes 589824 | tf_op jit(solution)/shard_map/reduce_scatter | solution.py:109
  683.6 369.2 %reduce-scatter.13.cloned.1.call-start = ((), (), s32[]{:S(2)}) async-start(), calls=%async_computation.8 | async-start | bytes 2162688 | tf_op jit(solution)/shard_map/reduce_scatter | solution.py:112
  689.9 598.0 %all-gather.5.cloned.1.call-start = ((), (), s32[]{:S(2)}) async-start(), calls=%async_computation.9 | async-start | bytes 1081344 | tf_op jit(solution)/shard_map/all_gather | solution.py:132
  1224.4 276.0 %reduce-scatter.15.cloned.1.call-start = ((), (), s32[]{:S(2)}) async-start(), calls=%async_computation.10 | async-start | bytes 589824 | tf_op jit(solution)/shard_map/reduce_scatter | solution.py:109
  1347.1 369.5 %reduce-scatter.17.cloned.1.call-start = ((), (), s32[]{:S(2)}) async-start(), calls=%async_computation.11 | async-start | bytes 2162688 | tf_op jit(solution)/shard_map/reduce_scatter | solution.py:112
Sparse Core Ops, SparseCore 0:
  228.2 93.4 reduce-scatter.18
  325.7 226.1 reduce-scatter.20
  555.2 69.4 all-gather.2
  683.8 153.1 reduce-scatter.10
  840.7 212.1 reduce-scatter.12
  1224.6 63.2 all-gather.4
  1347.2 153.1 reduce-scatter.14
  1504.2 212.2 reduce-scatter.16
where the time goes:
time: 1820 us; the launch traced here: 1810 us
  waiting for transfers between devices  1150 us (63%)
  blocking collectives  265 us (15%)
  other arithmetic  194 us (11%)
  matrix products  103 us (6%)
  local copies, waits for them, and re-layouts  88.3 us (5%)
    reduce_scatter x2, waiting for transfers between devices, partial_sums(): lax.psum_scatter(col_total.reshape(query_rows, col_blocks * 128), 'col',...  432 us
    unnamed x10, waiting for transfers between devices  318 us
    reduce_scatter x2, waiting for transfers between devices, partial_sums(): lax.psum_scatter(row_total.reshape(query_rows, row_blocks * 128), 'row',...  294 us
    dynamic_update_slice x16, other arithmetic, build_blocks(): lax.map(fill_group, (index_groups, value_groups))  160 us
    psum x2, blocking collectives, residual_gram(): return symmetric(lax.psum(gram_matrix(current, current), ('row', 'col')))  154 us
    all_gather x2, waiting for transfers between devices, body(): lax.all_gather(scaled, 'col', axis=1, tiled=True)  103 us
    psum x1, blocking collectives, body(): lax.psum(gram_matrix(direction, applied), ('row', 'col'))  79.9 us
    dot_general x15, matrix products, group_turn(): jnp.einsum('sb,msi->mbi', col_select, backward, precision=lax.Precision.H...  42.9 us
  transfers between devices with their start and end apart: 8, of which 8 were waited for; matrix products, arithmetic and copies ran while one was open for 1% of the time, Pallas kernels for 0%

commit v1 on v0

v1 whole, which is shorter than its diff:
```python
import functools

import jax
import jax.numpy as jnp
from jax import lax
from jax.experimental import pallas as pl
from jax.experimental.pallas import tpu as pltpu
from jax.sharding import PartitionSpec as P

MESH = pl.DeviceIdType.MESH
HIGH = lax.Precision.HIGHEST
F32 = jnp.float32
BF16 = jnp.bfloat16
WEIGHT = 0.95
PS = 4
UNROLL = 8


def mm(first, second, transposed=False):
    dims = (((1,), (1 if transposed else 0,)), ((), ()))
    return lax.dot_general(first, second, dims, preferred_element_type=F32)


def mm_high(first, second, transposed=False):
    dims = (((1,), (1 if transposed else 0,)), ((), ()))
    return lax.dot_general(first, second, dims, precision=HIGH, preferred_element_type=F32)


def lanes(*parts):
    width = sum(p.shape[1] for p in parts)
    return jnp.concatenate(list(parts) + [jnp.zeros((parts[0].shape[0], 128 - width), F32)], axis=1)


def tall(small):
    return jnp.concatenate([small, jnp.zeros((128 - small.shape[0], 128), F32)], axis=0)


def flip(small):
    return tall(small).T[0:32]


def symmetric(small):
    return 0.5 * (small + flip(small))


def small_mm(first, second):
    return mm_high(first, tall(second))


def inverse(small):
    size = small.shape[0]
    row_ids = lax.broadcasted_iota(jnp.int32, small.shape, 0)
    lane_ids = lax.broadcasted_iota(jnp.int32, small.shape, 1)
    both = small + (row_ids + size == lane_ids).astype(F32)
    for k in range(size):
        pivot_row = both[k : k + 1, :] / both[k : k + 1, k : k + 1]
        both = jnp.where(row_ids == k, pivot_row, both - both[:, k : k + 1] * pivot_row)
    return lanes(both[:, size : 2 * size])


def kernel(
    sizes, q_ref, spots_ref, spot_row_ref, live_ref, cols_ref, sims_ref, sol_ref, res_ref,
    blocks, colsum, rowsum, basis, scale,
    xc, xr, xc2, xr2, fwd, bwd, out_r, out_c, out_rb, out_cb,
    deg_r, deg_c, deg_rr, deg_cr, scl_r, scl_c,
    yr, zs, zr, rr, gram, gram_in,
    ag_s, ag_r, ag_ys, ag_yr, dg_s, dg_r, sc_s, sc_r, rs_s, rs_r, rs_ys, rs_yr, ar_s, ar_r,
):
    R, Y, Z = sizes
    C = Y * Z
    RB, CB = R * PS, C * PS
    SLOTS = blocks.shape[0]
    shift = CB.bit_length() - 1
    a = lax.axis_index("row")
    b = lax.axis_index("col")
    y = b // Z
    z = b % Z

    def row_dev(k):
        return (lax.rem(a + k, R), b)

    def col_dev(k):
        return (a, lax.rem(b + k, C))

    def z_dev(k):
        return (a, y * Z + lax.rem(z + k, Z))

    def y_dev(k):
        return (a, lax.rem(y + k, Y) * Z + z)

    def copy(src, dst, ss, rs, dev):
        return pltpu.make_async_remote_copy(
            src_ref=src, dst_ref=dst, send_sem=ss, recv_sem=rs, device_id=dev, device_id_type=MESH
        )

    barrier = pltpu.get_barrier_semaphore()
    for k in range(1, R):
        pl.semaphore_signal(barrier, inc=1, device_id=row_dev(k), device_id_type=MESH)
    for k in range(1, C):
        pl.semaphore_signal(barrier, inc=1, device_id=col_dev(k), device_id_type=MESH)
    pl.semaphore_wait(barrier, R - 1 + C - 1)

    class Gather:
        def __init__(self, turn, col_buf, row_buf):
            mine_c = col_buf.at[pl.ds(b * PS, PS)]
            mine_r = row_buf.at[pl.ds(a * PS, PS)]
            self.row = [
                copy(mine_r, mine_r, ag_s.at[turn, k], ag_r.at[turn, k], row_dev(k)) for k in range(1, R)
            ]
            self.z = [
                copy(mine_c, mine_c, ag_s.at[turn, R + k], ag_r.at[turn, R + k], z_dev(k))
                for k in range(1, Z)
            ]
            self.y = []
            for kz in range(Z):
                chunk = col_buf.at[pl.ds((y * Z + lax.rem(z - kz + Z, Z)) * PS, PS)]
                self.y.append(
                    [
                        copy(chunk, chunk, ag_ys.at[turn, kz, ky], ag_yr.at[turn, kz, ky], y_dev(ky))
                        for ky in range(1, Y)
                    ]
                )

        def start(self):
            for c in self.y[0] + self.z + self.row:
                c.start()

        def forward(self):
            for kz in range(1, Z):
                self.z[kz - 1].wait_recv()
                for c in self.y[kz]:
                    c.start()

        def finish(self):
            for c in self.row:
                c.wait()
            for c in self.z:
                c.wait_send()
            for group in self.y:
                for c in group:
                    c.wait()

    basis[32:128, :] = jnp.zeros((96, PS * 128), F32)
    for p in range(PS):
        part = q_ref[:, p * 128 : (p + 1) * 128]
        basis[0:32, p * 128 : (p + 1) * 128] = part
        xc[b * PS + p] = part.astype(BF16)
        xr[a * PS + p] = part.astype(BF16)
    gather1 = Gather(0, xc, xr)
    gather1.start()

    lane_ids = lax.broadcasted_iota(jnp.int32, (128, 128), 0).astype(jnp.int16)
    ones = jnp.ones((8, 128), BF16)

    def build(s):
        idx = cols_ref[s]
        sim = sims_ref[s].astype(F32)
        value = jnp.zeros(sim.shape, F32)
        for t in range(idx.shape[0]):
            value = value + jnp.where(idx == idx[t : t + 1], sim[t : t + 1], 0.0)
        value = value.astype(BF16)
        idx = idx.astype(jnp.int16)
        block = jnp.zeros((128, 128), BF16)
        for t in range(idx.shape[0]):
            here = lane_ids == jnp.broadcast_to(idx[t : t + 1], (128, 128))
            block = jnp.where(here, jnp.broadcast_to(value[t : t + 1], (128, 128)), block)
        blocks[s] = block
        rowsum[pl.ds(s, 1), :] = jnp.sum(sim, axis=0, keepdims=True)
        colsum[pl.ds(s, 1), :] = mm(ones, block, True)[0:1]

    def build_range(low, high):
        def turn(g, carry):
            for u in range(UNROLL):
                build(g * UNROLL + u)
            return carry

        lax.fori_loop(low // UNROLL, high // UNROLL, turn, 0)

    build_range(0, SLOTS // 2)
    gather1.forward()
    build_range(SLOTS // 2, SLOTS)

    spot_row = spot_row_ref[...]
    live = live_ref[0, 0]
    used = lax.broadcasted_iota(jnp.int32, (1, SLOTS), 1) < live
    in_row = (lax.shift_right_logical(spot_row, shift) == lax.broadcasted_iota(jnp.int32, (RB, SLOTS), 0)) & used
    in_col = ((spot_row & (CB - 1)) == lax.broadcasted_iota(jnp.int32, (CB, SLOTS), 0)) & used
    in_row_f = jnp.where(in_row, 1.0, 0.0).astype(F32)
    in_col_f = jnp.where(in_col, 1.0, 0.0).astype(F32)
    row_degree = mm_high(in_row_f, rowsum[...])
    col_degree = mm_high(in_col_f, colsum[...])
    for g in range(R):
        deg_r[g] = row_degree[g * PS : (g + 1) * PS]
    for g in range(C):
        deg_c[g] = col_degree[g * PS : (g + 1) * PS]
    sends = []
    for k in range(1, C):
        sends.append(copy(deg_c.at[lax.rem(b + k, C)], deg_cr.at[k], dg_s.at[k], dg_r.at[k], col_dev(k)))
    for k in range(1, R):
        sends.append(
            copy(deg_r.at[lax.rem(a + k, R)], deg_rr.at[k], dg_s.at[C + k], dg_r.at[C + k], row_dev(k))
        )
    for c in sends:
        c.start()
    degree = deg_r[a] + deg_c[b]
    for c in sends:
        c.wait()
    for k in range(1, C):
        degree = degree + deg_cr[k]
    for k in range(1, R):
        degree = degree + deg_rr[k]
    degree = 1.0 + 0.5 * degree
    scaling = 1.0 / jnp.sqrt(degree)
    scl_r[a] = scaling
    scl_c[b] = scaling
    scale[...] = scaling
    sends = []
    for k in range(1, C):
        sends.append(copy(scl_c.at[b], scl_c.at[b], sc_s.at[k], sc_r.at[k], col_dev(k)))
    for k in range(1, R):
        sends.append(copy(scl_r.at[a], scl_r.at[a], sc_s.at[C + k], sc_r.at[C + k], row_dev(k)))
    for c in sends:
        c.start()
    gather1.finish()
    for c in sends:
        c.wait()

    def scale_part(buf, scl, g):
        factors = scl[g]
        for p in range(PS):
            buf[g * PS + p] = (buf[g * PS + p].astype(F32) * factors[p : p + 1]).astype(BF16)

    def scale_cols(g, carry):
        scale_part(xc, scl_c, g)
        return carry

    def scale_rows(g, carry):
        scale_part(xr, scl_r, g)
        return carry

    lax.fori_loop(0, C, scale_cols, 0)
    lax.fori_loop(0, R, scale_rows, 0)

    def apply(col_buf, row_buf):
        def pair(s):
            spot0, spot1 = spots_ref[s], spots_ref[s + 1]
            block0, block1 = blocks[s], blocks[s + 1]
            c0, c1 = col_buf[spot0 & (CB - 1)], col_buf[spot1 & (CB - 1)]
            r0 = row_buf[lax.shift_right_logical(spot0, shift)]
            r1 = row_buf[lax.shift_right_logical(spot1, shift)]
            ahead = mm(jnp.concatenate([c0, c1], 0), jnp.concatenate([block0, block1], 1))
            back = mm(jnp.concatenate([r0, r1], 0), jnp.concatenate([block0, block1], 0), True)
            fwd[:, s, :] = ahead[0:32, 0:128]
            fwd[:, s + 1, :] = ahead[32:64, 128:256]
            bwd[:, s, :] = back[0:32, 0:128]
            bwd[:, s + 1, :] = back[32:64, 128:256]

        def turn(g, carry):
            for u in range(UNROLL):
                pair(g * (2 * UNROLL) + 2 * u)
            return carry

        lax.fori_loop(0, SLOTS // (2 * UNROLL), turn, 0)
        pick_r = in_row_f.astype(BF16)
        pick_c = in_col_f.astype(BF16)

        def gather_sum(pick, terms):
            high = terms.astype(BF16)
            low = (terms - high.astype(F32)).astype(BF16)
            return mm(pick, high) + mm(pick, low)

        for m in range(32):
            out_c[:, m, :] = gather_sum(pick_c, bwd[m])
            out_r[:, m, :] = gather_sum(pick_r, fwd[m])

        def to_wire_c(v, carry):
            for p in range(PS):
                out_cb[v * PS + p] = out_c[v * PS + p].astype(BF16)
            return carry

        def to_wire_r(v, carry):
            for p in range(PS):
                out_rb[v * PS + p] = out_r[v * PS + p].astype(BF16)
            return carry

        lax.fori_loop(0, C, to_wire_c, 0)
        lax.fori_loop(0, R, to_wire_r, 0)

    def scatter_sum(turn):
        chunks = [(lax.rem(z + kz, Z)) for kz in range(Z)]
        ysends = []
        for kz in list(range(1, Z)) + [0]:
            group = []
            for ky in range(1, Y):
                src = out_cb.at[pl.ds((lax.rem(y + ky, Y) * Z + chunks[kz]) * PS, PS)]
                c = copy(
                    src, yr.at[turn, ky, kz], rs_ys.at[turn, ky, kz], rs_yr.at[turn, ky, kz], y_dev(ky)
                )
                c.start()
                group.append(c)
            ysends.append((kz, group))
        rsends = []
        for k in range(1, R):
            src = out_rb.at[pl.ds(lax.rem(a + k, R) * PS, PS)]
            c = copy(src, rr.at[turn, k], rs_s.at[turn, k], rs_r.at[turn, k], row_dev(k))
            c.start()
            rsends.append(c)
        zsends = []
        own = None
        for kz, group in ysends:
            for c in group:
                c.wait_recv()
            total = out_c[pl.ds((y * Z + chunks[kz]) * PS, PS)]
            for ky in range(1, Y):
                total = total + yr[turn, ky, kz].astype(F32)
            if kz:
                zs[turn, kz] = total.astype(BF16)
                c = copy(
                    zs.at[turn, kz], zr.at[turn, kz], rs_s.at[turn, R + kz], rs_r.at[turn, R + kz], z_dev(kz)
                )
                c.start()
                zsends.append(c)
            else:
                own = total
        own = own + out_r[pl.ds(a * PS, PS)]
        for k, c in enumerate(rsends):
            c.wait_recv()
            own = own + rr[turn, k + 1].astype(F32)
        for k, c in enumerate(zsends):
            c.wait_recv()
            own = own + zr[turn, k + 1].astype(F32)
        for kz, group in ysends:
            for c in group:
                c.wait_send()
        for c in rsends + zsends:
            c.wait_send()
        return own

    class Reduce:
        def __init__(self, turn):
            self.turn = turn

        def start(self, stage, value):
            turn = self.turn
            count, dev = ((R, row_dev), (Z, z_dev), (Y, y_dev))[stage]
            gram[turn, stage] = value
            self.value = value
            self.sends = []
            for k in range(1, count):
                c = copy(
                    gram.at[turn, stage],
                    gram_in.at[turn, stage, k],
                    ar_s.at[turn, stage, k],
                    ar_r.at[turn, stage, k],
                    dev(k),
                )
                c.start()
                self.sends.append(c)

        def finish(self, stage):
            total = self.value
            for k, c in enumerate(self.sends):
                c.wait()
                total = total + gram_in[self.turn, stage, k + 1]
            return total

    apply(xc, xr)
    summed = scatter_sum(0)
    scaling = scale[...]
    for p in range(PS):
        u1 = (0.5 * WEIGHT) * scaling[p : p + 1] * summed[p]
        basis[32:64, p * 128 : (p + 1) * 128] = u1
        part = (scaling[p : p + 1] * u1).astype(BF16)
        xc2[b * PS + p] = part
        xr2[a * PS + p] = part
    gather2 = Gather(1, xc2, xr2)
    gather2.start()
    early = Reduce(0)
    g0 = mm_high(basis[0:64, :], basis[...], True)
    early.start(0, lanes(g0[0:32, 0:64], g0[32:64, 32:64]))
    gather2.forward()
    early.start(1, early.finish(0))
    gather2.finish()
    early.start(2, early.finish(1))

    apply(xc2, xr2)
    grams = early.finish(2)
    summed = scatter_sum(1)
    scaling = scale[...]
    for p in range(PS):
        u2 = (0.5 * WEIGHT) * scaling[p : p + 1] * summed[p]
        basis[64:96, p * 128 : (p + 1) * 128] = u2
    late = Reduce(1)
    g2 = mm_high(basis[0:64, :], basis[...], True)
    late.start(0, lanes(g2[0:32, 64:96], g2[32:64, 64:96]))

    g00 = symmetric(lanes(grams[:, 0:32]))
    g01 = lanes(grams[:, 32:64])
    g11 = symmetric(lanes(grams[:, 64:96]))
    s01 = symmetric(g01)
    inv_curve = inverse(g00 - s01)
    inv_gram = inverse(g00)
    p1 = small_mm(g00, inv_curve)
    p0 = -small_mm(s01, inv_curve)
    p0_t, p1_t = flip(p0), flip(p1)
    newgram = small_mm(small_mm(p0, g00), p0_t) + small_mm(small_mm(p1, g11), p1_t)
    newgram = symmetric(newgram + 2.0 * small_mm(small_mm(p0, g01), p1_t))
    d0 = p0 + small_mm(newgram, inv_gram)
    e0, e1, e2 = d0, p1 - d0, -p1
    direction = lanes(d0[:, 0:32], p1[:, 0:32])
    applied = lanes(e0[:, 0:32], e1[:, 0:32], e2[:, 0:32])
    applied_t = tall(applied).T

    late.start(1, late.finish(0))
    late.start(2, late.finish(1))
    last = late.finish(2)
    whole = jnp.concatenate(
        [
            lanes(g00[:, 0:32], g01[:, 0:32], last[:, 0:32]),
            lanes(flip(g01)[:, 0:32], g11[:, 0:32], last[:, 32:64]),
        ],
        axis=0,
    )
    curve = symmetric(small_mm(direction, mm_high(whole, applied_t)))
    steps = small_mm(newgram, inverse(curve))
    sol_coef = lanes(p1[:, 0:32]) + small_mm(steps, direction)
    res_coef = lanes(p0[:, 0:32], p1[:, 0:32]) - small_mm(steps, applied)
    coef = jnp.concatenate([sol_coef, res_coef], axis=0)
    for p in range(PS):
        both = mm_high(coef, basis[:, p * 128 : (p + 1) * 128])
        sol_ref[:, p * 128 : (p + 1) * 128] = both[0:32]
        res_ref[:, p * 128 : (p + 1) * 128] = both[32:64]


def split_col(count):
    return (4, count // 4) if count >= 16 else (2, count // 2)


def solution(mesh):
    R, C = mesh.shape["row"], mesh.shape["col"]
    Y, Z = split_col(C)
    RB, CB = R * PS, C * PS

    def body(queries, block_spots, live_blocks, neighbor_cols, neighbor_sims):
        slots = block_spots.shape[2]
        vmem = pltpu.VMEM
        sems = pltpu.SemaphoreType.DMA
        scratch = [
            vmem((slots, 128, 128), BF16), vmem((slots, 128), F32), vmem((slots, 128), F32),
            vmem((128, PS * 128), F32), vmem((PS, 128), F32),
            vmem((CB, 32, 128), BF16), vmem((RB, 32, 128), BF16),
            vmem((CB, 32, 128), BF16), vmem((RB, 32, 128), BF16),
            vmem((32, slots, 128), F32), vmem((32, slots, 128), F32),
            vmem((RB, 32, 128), F32), vmem((CB, 32, 128), F32),
            vmem((RB, 32, 128), BF16), vmem((CB, 32, 128), BF16),
            vmem((R, PS, 128), F32), vmem((C, PS, 128), F32),
            vmem((R, PS, 128), F32), vmem((C, PS, 128), F32),
            vmem((R, PS, 128), F32), vmem((C, PS, 128), F32),
            vmem((2, Y, Z, PS, 32, 128), BF16), vmem((2, Z, PS, 32, 128), BF16),
            vmem((2, Z, PS, 32, 128), BF16), vmem((2, R, PS, 32, 128), BF16),
            vmem((2, 3, 32, 128), F32), vmem((2, 3, max(R, Z), 32, 128), F32),
            sems((2, R + Z)), sems((2, R + Z)), sems((2, Z, Y)), sems((2, Z, Y)),
            sems((C + R,)), sems((C + R,)), sems((C + R,)), sems((C + R,)),
            sems((2, R + Z)), sems((2, R + Z)), sems((2, Y, Z)), sems((2, Y, Z)),
            sems((2, 3, max(R, Z))), sems((2, 3, max(R, Z))),
        ]
        in_vmem = pl.BlockSpec(memory_space=pltpu.VMEM)
        in_smem = pl.BlockSpec(memory_space=pltpu.SMEM)
        shape = jax.ShapeDtypeStruct(queries.shape, F32)
        return pl.pallas_call(
            functools.partial(kernel, (R, Y, Z)),
            out_shape=(shape, shape),
            in_specs=[in_vmem, in_smem, in_vmem, in_smem, in_vmem, in_vmem],
            out_specs=(in_vmem, in_vmem),
            scratch_shapes=scratch,
            compiler_params=pltpu.CompilerParams(
                collective_id=0, has_side_effects=True, vmem_limit_bytes=52 * 1024 * 1024
            ),
        )(
            queries,
            block_spots[0, 0],
            block_spots[0],
            live_blocks,
            neighbor_cols[0, 0],
            neighbor_sims[0, 0],
        )

    placed = (
        P(None, ("row", "col")),
        P("row", "col", None),
        P("row", "col"),
        P("row", "col", None, None, None),
        P("row", "col", None, None, None),
    )
    return jax.shard_map(
        body,
        mesh=mesh,
        in_specs=placed,
        out_specs=(P(None, ("row", "col")), P(None, ("row", "col"))),
        check_vma=False,
    )
```

time: 1820 us -> 148 us (0.08)
  waiting for transfers between devices: 1150 us -> 0 us
  blocking collectives: 265 us -> 0 us
  other arithmetic: 194 us -> 0 us
  Pallas kernels: 0 us -> 140 us
  matrix products: 103 us -> 0 us
  local copies, waits for them, and re-layouts: 88.3 us -> 4 us
    reduce_scatter x4 -> x0, waiting for transfers between devices: 726 us -> none  [the longest x2 432 us: partial_sums(): lax.psum_scatter(col_total.reshape(query_rows, col_blocks * 128), 'col',...]
    unnamed x10 -> x0, waiting for transfers between devices: 318 us -> none
    psum x3 -> x0, blocking collectives: 234 us -> none  [the longest x2 154 us: residual_gram(): return symmetric(lax.psum(gram_matrix(current, current), ('row', 'col')))]
    dynamic_update_slice x16 -> x0, other arithmetic: 160 us -> none  [build_blocks(): lax.map(fill_group, (index_groups, value_groups))]
    pallas_call x0 -> x1, Pallas kernels: none -> 140 us  [body(): pl.pallas_call(functools.partial(kernel, (R, Y, Z)), out_shape=(shape, sh...]
    all_gather x2 -> x0, waiting for transfers between devices: 103 us -> none  [body(): lax.all_gather(scaled, 'col', axis=1, tiled=True)]
    dot_general x69 -> x0, matrix products: 102 us -> none  [the longest x15 42.9 us: group_turn(): jnp.einsum('sb,msi->mbi', col_select, backward, precision=lax.Precision.H...]
    all_gather x2 -> x0, blocking collectives: 31.4 us -> none  [body(): lax.all_gather(scaled, 'row', axis=1, tiled=True)]
  transfers between devices with their start and end apart: 8 -> 0, of which waited for: 8 -> 0; matrix products, arithmetic and copies ran while one was open for 1% -> 0% of each run, Pallas kernels for 0% -> 0%
where the time goes in v1:
time: 148 us; the launch traced here: 146 us
  Pallas kernels  140 us (95%)
  local copies, waits for them, and re-layouts  4 us (3%)
    pallas_call x1, Pallas kernels, body(): pl.pallas_call(functools.partial(kernel, (R, Y, Z)), out_shape=(shape, sh...  140 us
    unnamed x8, local copies, waits for them, and re-layouts  4 us

profile of v1, /device:TPU:1, one launch (start us, length us, event | category | flops | bytes accessed | tf_op | source)
XLA Modules:
  0.0 145.6 jit_solution(15952693637963037751)
XLA Ops:
  1.3 0.0 copy-start
  1.3 1.2 copy-done
  2.5 0.0 copy-start.1
  2.5 0.8 copy-done.1
  3.3 0.0 copy-start.2
  3.3 0.7 copy-done.2
  4.0 140.3 %shard_map.68 = (f32[32,512]{1,0:T(8,128)S(1)}, f32[32,512]{1,0:T(8,128)S(1)}) custom-call(f32[32,512]{1,0:T(8,128)S(1)} %copy-done.1, s32[256]{0:T(256)S(1)} %bitcast.5, s32[1,256]{1,0:T(1,128)S(1)} %bitcast.6, s32[1,1]{1,0:T(1,128)S(6)} %copy.9.live_ref, s32[256,16,128]{2,1,0:T(8,128)} %bitcast.7, bf16[256,16,128]{2,1,0:T(8,128)(2,1)S(1)} %bitcast.4), custom_call_target="tpu_custom_call" | custom-call | tf_op jit(solution)/shard_map/pallas_call | solution.py:470
  144.3 0.6 copy.10
  144.9 0.6 copy.11
Async XLA Ops:
  1.3 1.2 copy-start
  2.5 0.8 copy-start.1
  3.3 0.7 copy-start.2

commit v2 on v1

v2 whole, which is shorter than its diff:
```python
import functools

import jax
import jax.numpy as jnp
from jax import lax
from jax.experimental import pallas as pl
from jax.experimental.pallas import tpu as pltpu
from jax.sharding import PartitionSpec as P

MESH = pl.DeviceIdType.MESH
HIGH = lax.Precision.HIGHEST
F32 = jnp.float32
BF16 = jnp.bfloat16
WEIGHT = 0.95
PS = 4
UNROLL = 8
BUILD = 16


def mm(first, second, transposed=False):
    dims = (((1,), (1 if transposed else 0,)), ((), ()))
    return lax.dot_general(first, second, dims, preferred_element_type=F32)


def mm_high(first, second, transposed=False):
    dims = (((1,), (1 if transposed else 0,)), ((), ()))
    return lax.dot_general(first, second, dims, precision=HIGH, preferred_element_type=F32)


def lanes(*parts):
    width = sum(p.shape[1] for p in parts)
    return jnp.concatenate(list(parts) + [jnp.zeros((parts[0].shape[0], 128 - width), F32)], axis=1)


def tall(small):
    return jnp.concatenate([small, jnp.zeros((128 - small.shape[0], small.shape[1]), F32)], axis=0)


def pack(square):
    return jnp.concatenate([square[8 * i : 8 * i + 8, 0:32] for i in range(4)], axis=1)


def unpack(packed):
    return lanes(jnp.concatenate([packed[:, 32 * i : 32 * i + 32] for i in range(4)], axis=0))


def wait_all(ref, sem):
    pltpu.make_async_copy(ref, ref, sem).wait()


def flip(small):
    return tall(small).T[0:32]


def symmetric(small):
    return 0.5 * (small + flip(small))


def small_mm(first, second):
    return mm_high(first, tall(second))


def inverse(small):
    size = small.shape[0]
    row_ids = lax.broadcasted_iota(jnp.int32, small.shape, 0)
    lane_ids = lax.broadcasted_iota(jnp.int32, small.shape, 1)
    both = small + (row_ids + size == lane_ids).astype(F32)
    for k in range(size):
        pivot_row = both[k : k + 1, :] / both[k : k + 1, k : k + 1]
        both = jnp.where(row_ids == k, pivot_row, both - both[:, k : k + 1] * pivot_row)
    return lanes(both[:, size : 2 * size])


def kernel(
    sizes, q_hbm, spots_ref, spot_row_hbm, live_ref, cols_hbm, sims_hbm, sol_ref, res_ref,
    q_ref, spot_row_ref, cols_ref, sims_ref, blocks, colsum, rowsum, basis, vectors, scale,
    xc, xr, xc2, xr2, fwd, bwd, out_r, out_c, out_rb, out_cb,
    deg_r, deg_c, deg_rr, deg_cr, scl_r, scl_c,
    yr, relay_in, relay_out, zs, zr, rr, gram_e, gram_ei, gram_l, gram_li,
    in_s, ag_z, ag_sem, dg_sem, sc_sem, rs_relay, rs_y, rs_sem, ar_sem,
):
    R, Y, Z = sizes
    C = Y * Z
    RB, CB = R * PS, C * PS
    SLOTS = blocks.shape[0]
    shift = CB.bit_length() - 1
    a = lax.axis_index("row")
    b = lax.axis_index("col")
    y = b // Z
    z = b % Z

    def row_dev(k):
        return (lax.rem(a + k, R), b)

    def col_dev(k):
        return (a, lax.rem(b + k, C))

    def z_dev(k):
        return (a, y * Z + lax.rem(z + k, Z))

    def y_dev(k):
        return (a, lax.rem(y + k, Y) * Z + z)

    def copy(src, dst, ss, rs, dev):
        return pltpu.make_async_remote_copy(
            src_ref=src, dst_ref=dst, send_sem=ss, recv_sem=rs, device_id=dev, device_id_type=MESH
        )

    barrier = pltpu.get_barrier_semaphore()
    for k in range(1, R):
        pl.semaphore_signal(barrier, inc=1, device_id=row_dev(k), device_id_type=MESH)
    for k in range(1, C):
        pl.semaphore_signal(barrier, inc=1, device_id=col_dev(k), device_id_type=MESH)

    quarter = SLOTS // 4
    loads = []
    for n in range(4):
        part = pl.ds(n * quarter, quarter)
        loads.append(
            (
                pltpu.make_async_copy(cols_hbm.at[part], cols_ref.at[part], in_s.at[n]),
                pltpu.make_async_copy(sims_hbm.at[part], sims_ref.at[part], in_s.at[4 + n]),
            )
        )
    others = (
        pltpu.make_async_copy(q_hbm, q_ref, in_s.at[8]),
        pltpu.make_async_copy(spot_row_hbm, spot_row_ref, in_s.at[9]),
    )
    for c in [*loads[0], *others, *loads[1], *loads[2], *loads[3]]:
        c.start()

    near_first = sorted(range(1, Z), key=lambda k: (min(k, Z - k), k))

    class Gather:
        def __init__(self, turn, col_buf, row_buf):
            self.turn, self.col_buf, self.row_buf = turn, col_buf, row_buf
            mine_c = col_buf.at[pl.ds(b * PS, PS)]
            mine_r = row_buf.at[pl.ds(a * PS, PS)]
            col_sent, row_sent, y_got, row_got = [ag_sem.at[turn, n] for n in range(4)]
            self.row = [copy(mine_r, mine_r, row_sent, row_got, row_dev(k)) for k in range(1, R)]
            self.z = {k: copy(mine_c, mine_c, col_sent, ag_z.at[turn, k], z_dev(k)) for k in range(1, Z)}
            self.y = {}
            for kz in range(Z):
                chunk = col_buf.at[pl.ds((y * Z + lax.rem(z - kz + Z, Z)) * PS, PS)]
                self.y[kz] = [
                    copy(chunk, chunk, col_sent, y_got, y_dev(ky)) for ky in ((2, 1, 3) if Y == 4 else (1,))
                ]

        def start(self):
            for c in self.y[0]:
                c.start()
            for kz in near_first:
                self.z[kz].start()
            for c in self.row:
                c.start()

        def forward(self):
            for kz in near_first:
                self.z[kz].wait_recv()
                for c in self.y[kz]:
                    c.start()

        def finish(self):
            col_sent, row_sent, y_got, row_got = [ag_sem.at[self.turn, n] for n in range(4)]
            wait_all(self.col_buf.at[pl.ds(0, (Y - 1) * Z * PS)], y_got)
            wait_all(self.row_buf.at[pl.ds(0, (R - 1) * PS)], row_got)
            wait_all(self.col_buf.at[pl.ds(0, (C - 1) * PS)], col_sent)
            wait_all(self.row_buf.at[pl.ds(0, (R - 1) * PS)], row_sent)

    gather1 = Gather(0, xc, xr)

    lane_ids = lax.broadcasted_iota(jnp.int32, (128, 128), 0).astype(jnp.int16)
    halves = (
        lax.broadcasted_iota(jnp.int32, (8, 256), 0)
        == lax.shift_right_logical(lax.broadcasted_iota(jnp.int32, (8, 256), 1), 7)
    )
    halves = jnp.where(halves, 1.0, 0.0).astype(BF16)

    def build(s):
        idx = cols_ref[s]
        sim = sims_ref[s].astype(F32)
        value = jnp.zeros(sim.shape, F32)
        for t in range(idx.shape[0]):
            value = value + jnp.where(idx == idx[t : t + 1], sim[t : t + 1], 0.0)
        value = value.astype(BF16)
        idx = idx.astype(jnp.int16)
        block = jnp.zeros((128, 128), BF16)
        for t in range(idx.shape[0]):
            here = lane_ids == jnp.broadcast_to(idx[t : t + 1], (128, 128))
            block = jnp.where(here, jnp.broadcast_to(value[t : t + 1], (128, 128)), block)
        blocks[s] = block
        rowsum[pl.ds(s, 1), :] = jnp.sum(sim, axis=0, keepdims=True)
        return block

    def build_turn(g, carry):
        turns = SLOTS // BUILD
        for n in range(4):

            @pl.when(g == n * turns // 4)
            def _():
                for c in loads[n]:
                    c.wait()

        @pl.when(g == turns * 7 // 16)
        def _():
            for c in others:
                c.wait()
            basis[32:128, :] = jnp.zeros((96, PS * 128), F32)
            for p in range(PS):
                part = q_ref[:, p * 128 : (p + 1) * 128]
                basis[0:32, p * 128 : (p + 1) * 128] = part
                xc[b * PS + p] = part.astype(BF16)
                xr[a * PS + p] = part.astype(BF16)
            pl.semaphore_wait(barrier, R - 1 + C - 1)
            gather1.start()

        @pl.when(g == turns * 12 // 16)
        def _():
            gather1.forward()

        for u in range(0, BUILD, 4):
            s = g * BUILD + u
            four = [build(s + v) for v in range(4)]
            pairs = jnp.concatenate(
                [jnp.concatenate([four[0], four[2]], 1), jnp.concatenate([four[1], four[3]], 1)], 0
            )
            sums = mm(halves, pairs, True)
            colsum[pl.ds(s, 1), :] = sums[0:1, 0:128]
            colsum[pl.ds(s + 1, 1), :] = sums[0:1, 128:256]
            colsum[pl.ds(s + 2, 1), :] = sums[1:2, 0:128]
            colsum[pl.ds(s + 3, 1), :] = sums[1:2, 128:256]
        return carry

    lax.fori_loop(0, SLOTS // BUILD, build_turn, 0)

    spot_row = spot_row_ref[...]
    live = live_ref[0, 0]
    used = lax.broadcasted_iota(jnp.int32, (1, SLOTS), 1) < live
    in_row = (lax.shift_right_logical(spot_row, shift) == lax.broadcasted_iota(jnp.int32, (RB, SLOTS), 0)) & used
    in_col = ((spot_row & (CB - 1)) == lax.broadcasted_iota(jnp.int32, (CB, SLOTS), 0)) & used
    in_row_f = jnp.where(in_row, 1.0, 0.0).astype(F32)
    in_col_f = jnp.where(in_col, 1.0, 0.0).astype(F32)
    row_degree = mm_high(in_row_f, rowsum[...])
    col_degree = mm_high(in_col_f, colsum[...])
    for g in range(R):
        deg_r[g] = row_degree[g * PS : (g + 1) * PS]
    for g in range(C):
        deg_c[g] = col_degree[g * PS : (g + 1) * PS]
    for k in range(1, C):
        copy(deg_c.at[lax.rem(b + k, C)], deg_cr.at[k], dg_sem.at[0], dg_sem.at[1], col_dev(k)).start()
    for k in range(1, R):
        copy(deg_r.at[lax.rem(a + k, R)], deg_rr.at[k], dg_sem.at[2], dg_sem.at[3], row_dev(k)).start()
    degree = deg_r[a] + deg_c[b]
    wait_all(deg_rr.at[pl.ds(1, R - 1)], dg_sem.at[3])
    wait_all(deg_cr.at[pl.ds(1, C - 1)], dg_sem.at[1])
    for k in range(1, C):
        degree = degree + deg_cr[k]
    for k in range(1, R):
        degree = degree + deg_rr[k]
    degree = 1.0 + 0.5 * degree
    scaling = 1.0 / jnp.sqrt(degree)
    scl_r[a] = scaling
    scl_c[b] = scaling
    scale[...] = scaling
    for k in range(1, C):
        copy(scl_c.at[b], scl_c.at[b], sc_sem.at[0], sc_sem.at[1], col_dev(k)).start()
    for k in range(1, R):
        copy(scl_r.at[a], scl_r.at[a], sc_sem.at[2], sc_sem.at[3], row_dev(k)).start()
    gather1.finish()
    wait_all(deg_rr.at[pl.ds(1, R - 1)], dg_sem.at[2])
    wait_all(deg_cr.at[pl.ds(1, C - 1)], dg_sem.at[0])
    for n in range(2):
        wait_all(scl_c.at[pl.ds(0, C - 1)], sc_sem.at[n])
        wait_all(scl_r.at[pl.ds(0, R - 1)], sc_sem.at[2 + n])

    def scale_part(buf, scl, g):
        factors = scl[g]
        for p in range(PS):
            buf[g * PS + p] = (buf[g * PS + p].astype(F32) * factors[p : p + 1]).astype(BF16)

    def scale_cols(g, carry):
        scale_part(xc, scl_c, g)
        return carry

    def scale_rows(g, carry):
        scale_part(xr, scl_r, g)
        return carry

    lax.fori_loop(0, C, scale_cols, 0)
    lax.fori_loop(0, R, scale_rows, 0)

    def apply(col_buf, row_buf):
        def pair(s):
            spot0, spot1 = spots_ref[s], spots_ref[s + 1]
            block0, block1 = blocks[s], blocks[s + 1]
            c0, c1 = col_buf[spot0 & (CB - 1)], col_buf[spot1 & (CB - 1)]
            r0 = row_buf[lax.shift_right_logical(spot0, shift)]
            r1 = row_buf[lax.shift_right_logical(spot1, shift)]
            ahead = mm(jnp.concatenate([c0, c1], 0), jnp.concatenate([block0, block1], 1))
            back = mm(jnp.concatenate([r0, r1], 0), jnp.concatenate([block0, block1], 0), True)
            fwd[:, s, :] = ahead[0:32, 0:128]
            fwd[:, s + 1, :] = ahead[32:64, 128:256]
            bwd[:, s, :] = back[0:32, 0:128]
            bwd[:, s + 1, :] = back[32:64, 128:256]

        def turn(g, carry):
            for u in range(UNROLL):
                pair(g * (2 * UNROLL) + 2 * u)
            return carry

        lax.fori_loop(0, SLOTS // (2 * UNROLL), turn, 0)
        pick_r = in_row_f.astype(BF16)
        pick_c = in_col_f.astype(BF16)

        def gather_sum(pick, terms):
            high = terms.astype(BF16)
            low = (terms - high.astype(F32)).astype(BF16)
            return mm(pick, high) + mm(pick, low)

        for m in range(32):
            out_c[:, m, :] = gather_sum(pick_c, bwd[m])

        def to_wire_c(v, carry):
            for p in range(2 * PS):
                out_cb[v * 2 * PS + p] = out_c[v * 2 * PS + p].astype(BF16)
            return carry

        lax.fori_loop(0, C // 2, to_wire_c, 0)

        def row_part():
            for m in range(32):
                out_r[:, m, :] = gather_sum(pick_r, fwd[m])
            for v in range(RB):
                out_rb[v] = out_r[v].astype(BF16)

        return row_part

    ways = (1, Y - 1) if Y == 4 else (1,)

    def relay_way(kz):
        return 0 if kz % 2 == 0 else 1

    def scatter_sum(turn, row_part, beside=None):
        places = [lax.rem(z + kz, Z) for kz in range(Z)]
        order = list(reversed(near_first)) + [0]
        y_sent, z_sent, z_got, row_sent, row_got = [rs_sem.at[turn, n] for n in range(5)]

        def part(ky, kz):
            return pl.ds((lax.rem(y + ky, Y) * Z + places[kz]) * PS, PS)

        def half(src, kz, w):
            copy(src, yr.at[turn, kz, w], y_sent, rs_y.at[turn, kz], y_dev(ways[w])).start()

        relays = {}
        if Y == 4:
            for kz in order:
                relays[kz] = copy(
                    out_cb.at[part(2, kz)],
                    relay_in.at[turn, kz],
                    y_sent,
                    rs_relay.at[turn, kz],
                    y_dev(ways[relay_way(kz)]),
                )
                relays[kz].start()
        for kz in order:
            for w, ky in enumerate(ways):
                if Y != 4 or w != relay_way(kz):
                    half(out_cb.at[part(ky, kz)], kz, w)
        row_part()
        for k in range(1, R):
            src = out_rb.at[pl.ds(lax.rem(a + k, R) * PS, PS)]
            copy(src, rr.at[turn, k], row_sent, row_got, row_dev(k)).start()
        result = beside() if beside else None
        if Y == 4:
            for kz in order:
                w = relay_way(kz)
                relays[kz].wait_recv()
                total = out_c[part(ways[w], kz)] + relay_in[turn, kz].astype(F32)
                relay_out[turn, kz] = total.astype(BF16)
                half(relay_out.at[turn, kz], kz, w)
        own = out_r[pl.ds(a * PS, PS)]
        for kz in order:
            total = out_c[part(0, kz)]
            wait_all(yr.at[turn, kz], rs_y.at[turn, kz])
            for w in range(len(ways)):
                total = total + yr[turn, kz, w].astype(F32)
            if kz:
                zs[turn, kz] = total.astype(BF16)
                copy(zs.at[turn, kz], zr.at[turn, kz], z_sent, z_got, z_dev(kz)).start()
            else:
                own = own + total
        wait_all(rr.at[turn, pl.ds(1, R - 1)], row_got)
        for k in range(1, R):
            own = own + rr[turn, k].astype(F32)
        wait_all(zr.at[turn, pl.ds(1, Z - 1)], z_got)
        for kz in range(1, Z):
            own = own + zr[turn, kz].astype(F32)
        wait_all(out_cb.at[pl.ds(0, (Y - 1) * Z * PS)], y_sent)
        wait_all(rr.at[turn, pl.ds(1, R - 1)], row_sent)
        wait_all(zr.at[turn, pl.ds(1, Z - 1)], z_sent)
        return own, result

    class Reduce:
        def __init__(self, turn, buf, buf_in):
            self.turn, self.buf, self.buf_in = turn, buf, buf_in

        def start(self, stage, value):
            count, dev = ((R, row_dev), (Z, z_dev), (Y, y_dev))[stage]
            self.buf[stage] = value
            for k in range(1, count):
                copy(
                    self.buf.at[stage],
                    self.buf_in.at[stage, k],
                    ar_sem.at[self.turn, stage, 0],
                    ar_sem.at[self.turn, stage, 1],
                    dev(k),
                ).start()

        def finish(self, stage):
            count = (R, Z, Y)[stage]
            there = self.buf_in.at[stage, pl.ds(1, count - 1)]
            wait_all(there, ar_sem.at[self.turn, stage, 1])
            total = self.buf[stage]
            for k in range(1, count):
                total = total + self.buf_in[stage, k]
            wait_all(there, ar_sem.at[self.turn, stage, 0])
            return total

    row_part = apply(xc, xr)
    summed, _ = scatter_sum(0, row_part)
    scaling = scale[...]
    for p in range(PS):
        u1 = (0.5 * WEIGHT) * scaling[p : p + 1] * summed[p]
        basis[32:64, p * 128 : (p + 1) * 128] = u1
        part = (scaling[p : p + 1] * u1).astype(BF16)
        xc2[b * PS + p] = part
        xr2[a * PS + p] = part
    gather2 = Gather(1, xc2, xr2)
    gather2.start()
    early = Reduce(0, gram_e, gram_ei)
    g0 = mm_high(basis[0:64, :], basis[0:64, :], True)
    early.start(
        0, jnp.concatenate([pack(g0[0:32]), pack(g0[0:32, 32:64]), pack(g0[32:64, 32:64])], axis=0)
    )
    gather2.forward()
    early.start(1, early.finish(0))
    gather2.finish()
    early.start(2, early.finish(1))

    def first_systems():
        grams = early.finish(2)
        g00 = symmetric(unpack(grams[0:8]))
        g01 = unpack(grams[8:16])
        g11 = symmetric(unpack(grams[16:24]))
        s01 = symmetric(g01)
        inv_curve = inverse(g00 - s01)
        inv_gram = inverse(g00)
        p1 = small_mm(g00, inv_curve)
        p0 = -small_mm(s01, inv_curve)
        p0_t, p1_t = flip(p0), flip(p1)
        newgram = small_mm(small_mm(p0, g00), p0_t) + small_mm(small_mm(p1, g11), p1_t)
        newgram = symmetric(newgram + 2.0 * small_mm(small_mm(p0, g01), p1_t))
        d0 = p0 + small_mm(newgram, inv_gram)
        direction = lanes(d0[:, 0:32], p1[:, 0:32])
        applied = lanes(d0[:, 0:32], p1[:, 0:32] - d0[:, 0:32], -p1[:, 0:32])
        whole = jnp.concatenate(
            [
                lanes(g00[:, 0:32], g01[:, 0:32], g11[:, 0:32]),
                lanes(flip(g01)[:, 0:32], g11[:, 0:32]),
            ],
            axis=0,
        )
        known = small_mm(direction, mm_high(whole, tall(applied).T))
        coef = jnp.concatenate([direction, lanes(p0[:, 0:32], p1[:, 0:32]), p1], axis=0)
        vectors[...] = mm_high(coef, basis[...])
        return newgram, p1, p1_t, applied, known

    row_part = apply(xc2, xr2)
    summed, small = scatter_sum(1, row_part, first_systems)
    newgram, p1, p1_t, applied, known = small
    scaling = scale[...]
    for p in range(PS):
        u2 = (0.5 * WEIGHT) * scaling[p : p + 1] * summed[p]
        basis[64:96, p * 128 : (p + 1) * 128] = u2
    late = Reduce(1, gram_l, gram_li)
    late.start(0, pack(mm_high(basis[32:64, :], basis[64:96, :], True)))
    image = mm_high(applied, basis[...])
    late.start(1, late.finish(0))
    late.start(2, late.finish(1))
    g12 = unpack(late.finish(2))
    curve = symmetric(known - small_mm(small_mm(p1, g12), p1_t))
    steps = small_mm(newgram, inverse(curve))
    sol_ref[...] = vectors[64:96, :] + mm_high(steps, tall(vectors[0:32, :]))
    res_ref[...] = vectors[32:64, :] - mm_high(steps, tall(image))


def split_col(count):
    return (4, count // 4) if count >= 8 else (2, count // 2)


def solution(mesh):
    R, C = mesh.shape["row"], mesh.shape["col"]
    Y, Z = split_col(C)
    RB, CB = R * PS, C * PS

    def body(queries, block_spots, live_blocks, neighbor_cols, neighbor_sims):
        slots = block_spots.shape[2]
        vmem = pltpu.VMEM
        sems = pltpu.SemaphoreType.DMA
        ways = 2 if Y == 4 else 1
        scratch = [
            vmem(queries.shape, F32), vmem((1, slots), jnp.int32),
            vmem(neighbor_cols.shape[2:], jnp.int32), vmem(neighbor_sims.shape[2:], BF16),
            vmem((slots, 128, 128), BF16), vmem((slots, 128), F32), vmem((slots, 128), F32),
            vmem((128, PS * 128), F32), vmem((96, PS * 128), F32), vmem((PS, 128), F32),
            vmem((CB, 32, 128), BF16), vmem((RB, 32, 128), BF16),
            vmem((CB, 32, 128), BF16), vmem((RB, 32, 128), BF16),
            vmem((32, slots, 128), F32), vmem((32, slots, 128), F32),
            vmem((RB, 32, 128), F32), vmem((CB, 32, 128), F32),
            vmem((RB, 32, 128), BF16), vmem((CB, 32, 128), BF16),
            vmem((R, PS, 128), F32), vmem((C, PS, 128), F32),
            vmem((R, PS, 128), F32), vmem((C, PS, 128), F32),
            vmem((R, PS, 128), F32), vmem((C, PS, 128), F32),
            vmem((2, Z, ways, PS, 32, 128), BF16), vmem((2, Z, PS, 32, 128), BF16),
            vmem((2, Z, PS, 32, 128), BF16), vmem((2, Z, PS, 32, 128), BF16),
            vmem((2, Z, PS, 32, 128), BF16), vmem((2, R, PS, 32, 128), BF16),
            vmem((3, 24, 128), F32), vmem((3, max(R, Z, Y), 24, 128), F32),
            vmem((3, 8, 128), F32), vmem((3, max(R, Z, Y), 8, 128), F32),
            sems((10,)), sems((2, Z)), sems((2, 4)), sems((4,)), sems((4,)),
            sems((2, Z)), sems((2, Z)), sems((2, 5)), sems((2, 3, 2)),
        ]
        in_vmem = pl.BlockSpec(memory_space=pltpu.VMEM)
        in_any = pl.BlockSpec(memory_space=pl.ANY)
        in_smem = pl.BlockSpec(memory_space=pltpu.SMEM)
        shape = jax.ShapeDtypeStruct(queries.shape, F32)
        return pl.pallas_call(
            functools.partial(kernel, (R, Y, Z)),
            out_shape=(shape, shape),
            in_specs=[in_any, in_smem, in_any, in_smem, in_any, in_any],
            out_specs=(in_vmem, in_vmem),
            scratch_shapes=scratch,
            compiler_params=pltpu.CompilerParams(
                collective_id=0, has_side_effects=True, vmem_limit_bytes=60 * 1024 * 1024
            ),
        )(
            queries,
            block_spots[0, 0],
            block_spots[0],
            live_blocks,
            neighbor_cols[0, 0],
            neighbor_sims[0, 0],
        )

    placed = (
        P(None, ("row", "col")),
        P("row", "col", None),
        P("row", "col"),
        P("row", "col", None, None, None),
        P("row", "col", None, None, None),
    )
    return jax.shard_map(
        body,
        mesh=mesh,
        in_specs=placed,
        out_specs=(P(None, ("row", "col")), P(None, ("row", "col"))),
        check_vma=False,
    )
```

time: 148 us -> 130 us (0.88)
  Pallas kernels: 140 us -> 125 us
    pallas_call x1, Pallas kernels: 140 us -> 125 us  [body(): pl.pallas_call(functools.partial(kernel, (R, Y, Z)), out_shape=(shape, sh...]
    unnamed x8 -> x2, local copies, waits for them, and re-layouts: 4 us -> 2.95 us
where the time goes in v2:
time: 130 us; the launch traced here: 129 us
  Pallas kernels  125 us (96%)
  local copies, waits for them, and re-layouts  2.95 us (2%)
    pallas_call x1, Pallas kernels, body(): pl.pallas_call(functools.partial(kernel, (R, Y, Z)), out_shape=(shape, sh...  125 us
    unnamed x2, local copies, waits for them, and re-layouts  2.95 us

profile of v2, /device:TPU:1, one launch (start us, length us, event | category | flops | bytes accessed | tf_op | source)
XLA Modules:
  0.0 129.0 jit_solution(14489996008178831812)
XLA Ops:
  1.3 124.8 %shard_map.68 = (f32[32,512]{1,0:T(8,128)}, f32[32,512]{1,0:T(8,128)}) custom-call(f32[32,512]{1,0:T(8,128)} %q_hbm.1, s32[256]{0:T(256)} %bitcast.6, s32[1,256]{1,0:T(1,128)} %bitcast.7, s32[1,1]{1,0:T(1,128)S(6)} %copy.9.live_ref, s32[256,16,128]{2,1,0:T(8,128)} %bitcast.4, bf16[256,16,128]{2,1,0:T(8,128)(2,1)} %bitcast.5), custom_call_target="tpu_custom_call" | custom-call | tf_op jit(solution)/shard_map/pallas_call | solution.py:536
  126.1 1.5 %copy.10 = f32[32,512]{1,0:T(8,128)} copy(f32[32,512]{1,0:T(8,128)} %get-tuple-element.4) | data formatting | bytes 131072
  127.5 1.5 %copy.11 = f32[32,512]{1,0:T(8,128)} copy(f32[32,512]{1,0:T(8,128)} %get-tuple-element.5) | data formatting | bytes 131072

commit v3 on v2

--- a/solution.py
+++ b/solution.py
@@ -13,7 +13,7 @@
 BF16 = jnp.bfloat16
 WEIGHT = 0.95
 PS = 4
-UNROLL = 8
+UNROLL = 4
 BUILD = 16
 
 
@@ -126,7 +126,7 @@
         pltpu.make_async_copy(q_hbm, q_ref, in_s.at[8]),
         pltpu.make_async_copy(spot_row_hbm, spot_row_ref, in_s.at[9]),
     )
-    for c in [*loads[0], *others, *loads[1], *loads[2], *loads[3]]:
+    for c in [*others, *loads[0], *loads[1], *loads[2], *loads[3]]:
         c.start()
 
     near_first = sorted(range(1, Z), key=lambda k: (min(k, Z - k), k))
@@ -160,12 +160,13 @@
                 for c in self.y[kz]:
                     c.start()
 
-        def finish(self):
-            col_sent, row_sent, y_got, row_got = [ag_sem.at[self.turn, n] for n in range(4)]
-            wait_all(self.col_buf.at[pl.ds(0, (Y - 1) * Z * PS)], y_got)
-            wait_all(self.row_buf.at[pl.ds(0, (R - 1) * PS)], row_got)
-            wait_all(self.col_buf.at[pl.ds(0, (C - 1) * PS)], col_sent)
-            wait_all(self.row_buf.at[pl.ds(0, (R - 1) * PS)], row_sent)
+        def finish_row(self):
+            wait_all(self.row_buf.at[pl.ds(0, (R - 1) * PS)], ag_sem.at[self.turn, 3])
+            wait_all(self.row_buf.at[pl.ds(0, (R - 1) * PS)], ag_sem.at[self.turn, 1])
+
+        def finish_col(self):
+            wait_all(self.col_buf.at[pl.ds(0, (Y - 1) * Z * PS)], ag_sem.at[self.turn, 2])
+            wait_all(self.col_buf.at[pl.ds(0, (C - 1) * PS)], ag_sem.at[self.turn, 0])
 
     gather1 = Gather(0, xc, xr)
 
@@ -201,20 +202,7 @@
                 for c in loads[n]:
                     c.wait()
 
-        @pl.when(g == turns * 7 // 16)
-        def _():
-            for c in others:
-                c.wait()
-            basis[32:128, :] = jnp.zeros((96, PS * 128), F32)
-            for p in range(PS):
-                part = q_ref[:, p * 128 : (p + 1) * 128]
-                basis[0:32, p * 128 : (p + 1) * 128] = part
-                xc[b * PS + p] = part.astype(BF16)
-                xr[a * PS + p] = part.astype(BF16)
-            pl.semaphore_wait(barrier, R - 1 + C - 1)
-            gather1.start()
-
-        @pl.when(g == turns * 12 // 16)
+        @pl.when(g == turns // 2)
         def _():
             gather1.forward()
 
@@ -231,6 +219,16 @@
             colsum[pl.ds(s + 3, 1), :] = sums[1:2, 128:256]
         return carry
 
+    for c in others:
+        c.wait()
+    basis[32:128, :] = jnp.zeros((96, PS * 128), F32)
+    for p in range(PS):
+        part = q_ref[:, p * 128 : (p + 1) * 128]
+        basis[0:32, p * 128 : (p + 1) * 128] = part
+        xc[b * PS + p] = part.astype(BF16)
+        xr[a * PS + p] = part.astype(BF16)
+    pl.semaphore_wait(barrier, R - 1 + C - 1)
+    gather1.start()
     lax.fori_loop(0, SLOTS // BUILD, build_turn, 0)
 
     spot_row = spot_row_ref[...]
@@ -266,11 +264,10 @@
         copy(scl_c.at[b], scl_c.at[b], sc_sem.at[0], sc_sem.at[1], col_dev(k)).start()
     for k in range(1, R):
         copy(scl_r.at[a], scl_r.at[a], sc_sem.at[2], sc_sem.at[3], row_dev(k)).start()
-    gather1.finish()
+    gather1.finish_row()
     wait_all(deg_rr.at[pl.ds(1, R - 1)], dg_sem.at[2])
     wait_all(deg_cr.at[pl.ds(1, C - 1)], dg_sem.at[0])
     for n in range(2):
-        wait_all(scl_c.at[pl.ds(0, C - 1)], sc_sem.at[n])
         wait_all(scl_r.at[pl.ds(0, R - 1)], sc_sem.at[2 + n])
 
     def scale_part(buf, scl, g):
@@ -286,78 +283,83 @@
         scale_part(xr, scl_r, g)
         return carry
 
-    lax.fori_loop(0, C, scale_cols, 0)
     lax.fori_loop(0, R, scale_rows, 0)
 
-    def apply(col_buf, row_buf):
-        def pair(s):
-            spot0, spot1 = spots_ref[s], spots_ref[s + 1]
-            block0, block1 = blocks[s], blocks[s + 1]
-            c0, c1 = col_buf[spot0 & (CB - 1)], col_buf[spot1 & (CB - 1)]
-            r0 = row_buf[lax.shift_right_logical(spot0, shift)]
-            r1 = row_buf[lax.shift_right_logical(spot1, shift)]
-            ahead = mm(jnp.concatenate([c0, c1], 0), jnp.concatenate([block0, block1], 1))
-            back = mm(jnp.concatenate([r0, r1], 0), jnp.concatenate([block0, block1], 0), True)
-            fwd[:, s, :] = ahead[0:32, 0:128]
-            fwd[:, s + 1, :] = ahead[32:64, 128:256]
-            bwd[:, s, :] = back[0:32, 0:128]
-            bwd[:, s + 1, :] = back[32:64, 128:256]
-
+    def spread(x):
+        zero = jnp.zeros((32, 128), BF16)
+        pairs = [(x[0], zero), (x[1], zero), (zero, x[2]), (zero, x[3])]
+        return jnp.concatenate([jnp.concatenate(pair, 1) for pair in pairs], 0)
+
+    def square(x):
+        return jnp.concatenate([jnp.concatenate(x[0:2], 1), jnp.concatenate(x[2:4], 1)], 0)
+
+    def back_four(s, row_buf):
+        x = [row_buf[lax.shift_right_logical(spots_ref[s + n], shift)] for n in range(4)]
+        out = mm(spread(x), square([blocks[s], blocks[s + 2], blocks[s + 1], blocks[s + 3]]), True)
+        for n in range(4):
+            bwd[:, s + n, :] = out[32 * n : 32 * n + 32, 128 * (n & 1) : 128 * (n & 1) + 128]
+
+    def ahead_four(s, col_buf):
+        x = [col_buf[spots_ref[s + n] & (CB - 1)] for n in range(4)]
+        out = mm(spread(x), square([blocks[s + n] for n in range(4)]))
+        for n in range(4):
+            fwd[:, s + n, :] = out[32 * n : 32 * n + 32, 128 * (n & 1) : 128 * (n & 1) + 128]
+
+    def products(four, buf, low, high):
         def turn(g, carry):
             for u in range(UNROLL):
-                pair(g * (2 * UNROLL) + 2 * u)
+                four((g * UNROLL + u) * 4, buf)
             return carry
 
-        lax.fori_loop(0, SLOTS // (2 * UNROLL), turn, 0)
-        pick_r = in_row_f.astype(BF16)
-        pick_c = in_col_f.astype(BF16)
-
-        def gather_sum(pick, terms):
-            high = terms.astype(BF16)
-            low = (terms - high.astype(F32)).astype(BF16)
-            return mm(pick, high) + mm(pick, low)
-
+        lax.fori_loop(low // (4 * UNROLL), high // (4 * UNROLL), turn, 0)
+
+    pick_r = in_row_f.astype(BF16)
+    pick_c = in_col_f.astype(BF16)
+
+    def gather_sum(pick, terms):
+        high = terms.astype(BF16)
+        low = (terms - high.astype(F32)).astype(BF16)
+        return mm(pick, high) + mm(pick, low)
+
+    def col_part():
         for m in range(32):
             out_c[:, m, :] = gather_sum(pick_c, bwd[m])
 
-        def to_wire_c(v, carry):
+        def to_wire(v, carry):
             for p in range(2 * PS):
                 out_cb[v * 2 * PS + p] = out_c[v * 2 * PS + p].astype(BF16)
             return carry
 
-        lax.fori_loop(0, C // 2, to_wire_c, 0)
-
-        def row_part():
-            for m in range(32):
-                out_r[:, m, :] = gather_sum(pick_r, fwd[m])
-            for v in range(RB):
-                out_rb[v] = out_r[v].astype(BF16)
-
-        return row_part
+        lax.fori_loop(0, C // 2, to_wire, 0)
+
+    def row_part():
+        for m in range(32):
+            out_r[:, m, :] = gather_sum(pick_r, fwd[m])
+        for v in range(RB):
+            out_rb[v] = out_r[v].astype(BF16)
 
     ways = (1, Y - 1) if Y == 4 else (1,)
 
     def relay_way(kz):
         return 0 if kz % 2 == 0 else 1
 
-    def scatter_sum(turn, row_part, beside=None):
-        places = [lax.rem(z + kz, Z) for kz in range(Z)]
-        order = list(reversed(near_first)) + [0]
-        y_sent, z_sent, z_got, row_sent, row_got = [rs_sem.at[turn, n] for n in range(5)]
-
-        def part(ky, kz):
-            return pl.ds((lax.rem(y + ky, Y) * Z + places[kz]) * PS, PS)
-
-        def half(src, kz, w):
-            copy(src, yr.at[turn, kz, w], y_sent, rs_y.at[turn, kz], y_dev(ways[w])).start()
-
+    places = [lax.rem(z + kz, Z) for kz in range(Z)]
+    order = list(reversed(near_first)) + [0]
+
+    def target(ky, kz):
+        return pl.ds((lax.rem(y + ky, Y) * Z + places[kz]) * PS, PS)
+
+    def half(turn, src, kz, w):
+        copy(src, yr.at[turn, kz, w], rs_sem.at[turn, 0], rs_y.at[turn, kz], y_dev(ways[w])).start()
+
+    def start_col_sum(turn):
         relays = {}
         if Y == 4:
             for kz in order:
                 relays[kz] = copy(
-                    out_cb.at[part(2, kz)],
+                    out_cb.at[target(2, kz)],
                     relay_in.at[turn, kz],
-                    y_sent,
+                    rs_sem.at[turn, 0],
                     rs_relay.at[turn, kz],
                     y_dev(ways[relay_way(kz)]),
                 )
@@ -365,22 +367,28 @@
         for kz in order:
             for w, ky in enumerate(ways):
                 if Y != 4 or w != relay_way(kz):
-                    half(out_cb.at[part(ky, kz)], kz, w)
-        row_part()
+                    half(turn, out_cb.at[target(ky, kz)], kz, w)
+        return relays
+
+    def start_row_sum(turn):
         for k in range(1, R):
             src = out_rb.at[pl.ds(lax.rem(a + k, R) * PS, PS)]
-            copy(src, rr.at[turn, k], row_sent, row_got, row_dev(k)).start()
-        result = beside() if beside else None
+            copy(src, rr.at[turn, k], rs_sem.at[turn, 3], rs_sem.at[turn, 4], row_dev(k)).start()
+
+    def finish_sums(turn, relays, beside=(None, None)):
+        y_sent, z_sent, z_got, row_sent, row_got = [rs_sem.at[turn, n] for n in range(5)]
         if Y == 4:
             for kz in order:
                 w = relay_way(kz)
                 relays[kz].wait_recv()
-                total = out_c[part(ways[w], kz)] + relay_in[turn, kz].astype(F32)
+                total = out_c[target(ways[w], kz)] + relay_in[turn, kz].astype(F32)
                 relay_out[turn, kz] = total.astype(BF16)
-                half(relay_out.at[turn, kz], kz, w)
+                half(turn, relay_out.at[turn, kz], kz, w)
+        if beside[0]:
+            beside[0]()
         own = out_r[pl.ds(a * PS, PS)]
         for kz in order:
-            total = out_c[part(0, kz)]
+            total = out_c[target(0, kz)]
             wait_all(yr.at[turn, kz], rs_y.at[turn, kz])
             for w in range(len(ways)):
                 total = total + yr[turn, kz, w].astype(F32)
@@ -389,6 +397,7 @@
                 copy(zs.at[turn, kz], zr.at[turn, kz], z_sent, z_got, z_dev(kz)).start()
             else:
                 own = own + total
+        result = beside[1]() if beside[1] else None
         wait_all(rr.at[turn, pl.ds(1, R - 1)], row_got)
         for k in range(1, R):
             own = own + rr[turn, k].astype(F32)
@@ -426,8 +435,17 @@
             wait_all(there, ar_sem.at[self.turn, stage, 0])
             return total
 
-    row_part = apply(xc, xr)
-    summed, _ = scatter_sum(0, row_part)
+    products(back_four, xr, 0, SLOTS)
+    col_part()
+    relays = start_col_sum(0)
+    for n in range(2):
+        wait_all(scl_c.at[pl.ds(0, C - 1)], sc_sem.at[n])
+    gather1.finish_col()
+    lax.fori_loop(0, C, scale_cols, 0)
+    products(ahead_four, xc, 0, SLOTS)
+    row_part()
+    start_row_sum(0)
+    summed, _ = finish_sums(0, relays)
     scaling = scale[...]
     for p in range(PS):
         u1 = (0.5 * WEIGHT) * scaling[p : p + 1] * summed[p]
@@ -442,12 +460,22 @@
     early.start(
         0, jnp.concatenate([pack(g0[0:32]), pack(g0[0:32, 32:64]), pack(g0[32:64, 32:64])], axis=0)
     )
+    gather2.finish_row()
+    products(back_four, xr2, 0, SLOTS // 2)
     gather2.forward()
     early.start(1, early.finish(0))
-    gather2.finish()
+    products(back_four, xr2, SLOTS // 2, SLOTS)
+    col_part()
+    relays = start_col_sum(1)
     early.start(2, early.finish(1))
-
-    def first_systems():
+    gather2.finish_col()
+    products(ahead_four, xc2, 0, SLOTS)
+    row_part()
+    start_row_sum(1)
+
+    held = {}
+
+    def first_inverses():
         grams = early.finish(2)
         g00 = symmetric(unpack(grams[0:8]))
         g01 = unpack(grams[8:16])
@@ -455,6 +483,10 @@
         s01 = symmetric(g01)
         inv_curve = inverse(g00 - s01)
         inv_gram = inverse(g00)
+        held["all"] = g00, g01, g11, s01, inv_curve, inv_gram
+
+    def first_systems():
+        g00, g01, g11, s01, inv_curve, inv_gram = held["all"]
         p1 = small_mm(g00, inv_curve)
         p0 = -small_mm(s01, inv_curve)
         p0_t, p1_t = flip(p0), flip(p1)
@@ -475,8 +507,7 @@
         vectors[...] = mm_high(coef, basis[...])
         return newgram, p1, p1_t, applied, known
 
-    row_part = apply(xc2, xr2)
-    summed, small = scatter_sum(1, row_part, first_systems)
+    summed, small = finish_sums(1, relays, (first_inverses, first_systems))
     newgram, p1, p1_t, applied, known = small
     scaling = scale[...]
     for p in range(PS):
@@ -540,7 +571,7 @@
             out_specs=(in_vmem, in_vmem),
             scratch_shapes=scratch,
             compiler_params=pltpu.CompilerParams(
-                collective_id=0, has_side_effects=True, vmem_limit_bytes=60 * 1024 * 1024
+                collective_id=0, has_side_effects=True, vmem_limit_bytes=53 * 1024 * 1024 + 512 * 1024
             ),
         )(
             queries,

time: 130 us -> 123 us (0.946)
  Pallas kernels: 125 us -> 119 us
    pallas_call x1, Pallas kernels: 125 us -> 119 us  [body(): pl.pallas_call(functools.partial(kernel, (R, Y, Z)), out_shape=(shape, sh...]
    unnamed x2 -> x6, local copies, waits for them, and re-layouts: 2.95 us -> 2.77 us
where the time goes in v3:
time: 123 us
  Pallas kernels  119 us (97%)
  local copies, waits for them, and re-layouts  2.77 us (2%)
  between operations  1.29 us (1%)
    pallas_call x1, Pallas kernels, body(): pl.pallas_call(functools.partial(kernel, (R, Y, Z)), out_shape=(shape, sh...  119 us
    unnamed x6, local copies, waits for them, and re-layouts  2.77 us

profile of v3, /device:TPU:1, one launch (start us, length us, event | category | flops | bytes accessed | tf_op | source)
XLA Modules:
  0.0 123.1 jit_solution(15245836656346394298)
XLA Ops:
  1.3 0.0 copy-start
  1.3 0.8 copy-done
  2.1 0.0 copy-start.1
  2.1 0.7 copy-done.1
  2.8 119.1 %shard_map.68 = (f32[32,512]{1,0:T(8,128)S(1)}, f32[32,512]{1,0:T(8,128)S(1)}) custom-call(f32[32,512]{1,0:T(8,128)S(1)} %copy-done, s32[256]{0:T(256)S(1)} %bitcast.4, s32[1,256]{1,0:T(1,128)S(1)} %bitcast.5, s32[1,1]{1,0:T(1,128)S(6)} %copy.9.live_ref, s32[256,16,128]{2,1,0:T(8,128)} %bitcast.6, bf16[256,16,128]{2,1,0:T(8,128)(2,1)} %bitcast.7), custom_call_target="tpu_custom_call" | custom-call | tf_op jit(solution)/shard_map/pallas_call | solution.py:567
  121.9 0.6 copy.10
  122.5 0.6 copy.11
Async XLA Ops:
  1.3 0.8 copy-start
  2.1 0.7 copy-start.1

commit v4 on v3

--- a/solution.py
+++ b/solution.py
@@ -154,8 +154,8 @@
             for c in self.row:
                 c.start()
 
-        def forward(self):
-            for kz in near_first:
+        def forward(self, first=0, last=None):
+            for kz in near_first[first:last]:
                 self.z[kz].wait_recv()
                 for c in self.y[kz]:
                     c.start()
@@ -260,10 +260,10 @@
     scl_r[a] = scaling
     scl_c[b] = scaling
     scale[...] = scaling
+    for k in range(1, R):
+        copy(scl_r.at[a], scl_r.at[a], sc_sem.at[2], sc_sem.at[3], row_dev(k)).start()
     for k in range(1, C):
         copy(scl_c.at[b], scl_c.at[b], sc_sem.at[0], sc_sem.at[1], col_dev(k)).start()
-    for k in range(1, R):
-        copy(scl_r.at[a], scl_r.at[a], sc_sem.at[2], sc_sem.at[3], row_dev(k)).start()
     gather1.finish_row()
     wait_all(deg_rr.at[pl.ds(1, R - 1)], dg_sem.at[2])
     wait_all(deg_cr.at[pl.ds(1, C - 1)], dg_sem.at[0])
@@ -375,18 +375,15 @@
             src = out_rb.at[pl.ds(lax.rem(a + k, R) * PS, PS)]
             copy(src, rr.at[turn, k], rs_sem.at[turn, 3], rs_sem.at[turn, 4], row_dev(k)).start()
 
-    def finish_sums(turn, relays, beside=(None, None)):
-        y_sent, z_sent, z_got, row_sent, row_got = [rs_sem.at[turn, n] for n in range(5)]
-        if Y == 4:
-            for kz in order:
-                w = relay_way(kz)
-                relays[kz].wait_recv()
-                total = out_c[target(ways[w], kz)] + relay_in[turn, kz].astype(F32)
-                relay_out[turn, kz] = total.astype(BF16)
-                half(turn, relay_out.at[turn, kz], kz, w)
-        if beside[0]:
-            beside[0]()
-        own = out_r[pl.ds(a * PS, PS)]
+    def hand_on(turn, relays):
+        for kz in relays:
+            w = relay_way(kz)
+            relays[kz].wait_recv()
+            total = out_c[target(ways[w], kz)] + relay_in[turn, kz].astype(F32)
+            relay_out[turn, kz] = total.astype(BF16)
+            half(turn, relay_out.at[turn, kz], kz, w)
+
+    def start_z_sum(turn):
         for kz in order:
             total = out_c[target(0, kz)]
             wait_all(yr.at[turn, kz], rs_y.at[turn, kz])
@@ -394,20 +391,24 @@
                 total = total + yr[turn, kz, w].astype(F32)
             if kz:
                 zs[turn, kz] = total.astype(BF16)
-                copy(zs.at[turn, kz], zr.at[turn, kz], z_sent, z_got, z_dev(kz)).start()
-            else:
-                own = own + total
-        result = beside[1]() if beside[1] else None
+                copy(
+                    zs.at[turn, kz], zr.at[turn, kz], rs_sem.at[turn, 1], rs_sem.at[turn, 2], z_dev(kz)
+                ).start()
+        return total
+
+    def finish_sums(turn, own):
+        y_sent, z_sent, z_got, row_sent, row_got = [rs_sem.at[turn, n] for n in range(5)]
+        own = own + out_r[pl.ds(a * PS, PS)]
+        wait_all(zr.at[turn, pl.ds(1, Z - 1)], z_got)
+        for kz in range(1, Z):
+            own = own + zr[turn, kz].astype(F32)
         wait_all(rr.at[turn, pl.ds(1, R - 1)], row_got)
         for k in range(1, R):
             own = own + rr[turn, k].astype(F32)
-        wait_all(zr.at[turn, pl.ds(1, Z - 1)], z_got)
-        for kz in range(1, Z):
-            own = own + zr[turn, kz].astype(F32)
         wait_all(out_cb.at[pl.ds(0, (Y - 1) * Z * PS)], y_sent)
         wait_all(rr.at[turn, pl.ds(1, R - 1)], row_sent)
         wait_all(zr.at[turn, pl.ds(1, Z - 1)], z_sent)
-        return own, result
+        return own
 
     class Reduce:
         def __init__(self, turn, buf, buf_in):
@@ -442,10 +443,12 @@
         wait_all(scl_c.at[pl.ds(0, C - 1)], sc_sem.at[n])
     gather1.finish_col()
     lax.fori_loop(0, C, scale_cols, 0)
-    products(ahead_four, xc, 0, SLOTS)
+    products(ahead_four, xc, 0, SLOTS // 2)
+    hand_on(0, relays)
+    products(ahead_four, xc, SLOTS // 2, SLOTS)
     row_part()
     start_row_sum(0)
-    summed, _ = finish_sums(0, relays)
+    summed = finish_sums(0, start_z_sum(0))
     scaling = scale[...]
     for p in range(PS):
         u1 = (0.5 * WEIGHT) * scaling[p : p + 1] * summed[p]
@@ -460,18 +463,17 @@
     early.start(
         0, jnp.concatenate([pack(g0[0:32]), pack(g0[0:32, 32:64]), pack(g0[32:64, 32:64])], axis=0)
     )
+    gather2.forward(0, 2)
     gather2.finish_row()
-    products(back_four, xr2, 0, SLOTS // 2)
-    gather2.forward()
+    products(back_four, xr2, 0, SLOTS // 4)
+    gather2.forward(2, 4)
+    products(back_four, xr2, SLOTS // 4, SLOTS // 2)
+    gather2.forward(4)
     early.start(1, early.finish(0))
     products(back_four, xr2, SLOTS // 2, SLOTS)
     col_part()
     relays = start_col_sum(1)
     early.start(2, early.finish(1))
-    gather2.finish_col()
-    products(ahead_four, xc2, 0, SLOTS)
-    row_part()
-    start_row_sum(1)
 
     held = {}
 
@@ -507,21 +509,39 @@
         vectors[...] = mm_high(coef, basis[...])
         return newgram, p1, p1_t, applied, known
 
-    summed, small = finish_sums(1, relays, (first_inverses, first_systems))
-    newgram, p1, p1_t, applied, known = small
+    gather2.finish_col()
+
+    def add_share(g, total):
+        for n in range(0, 2 * PS, 2):
+            v = g * 2 * PS + n
+            here = jnp.concatenate([xc2[v], xc2[v + 1]], axis=1)
+            there = jnp.concatenate([out_cb[v], out_cb[v + 1]], axis=1)
+            total = total + mm(here, there, True)
+        return total
+
+    share = lax.fori_loop(0, C // 2, add_share, jnp.zeros((32, 32), F32))
+    late = Reduce(1, gram_l, gram_li)
+    late.start(0, pack(WEIGHT * share))
+    products(ahead_four, xc2, 0, SLOTS // 2)
+    hand_on(1, relays)
+    late.start(1, late.finish(0))
+    products(ahead_four, xc2, SLOTS // 2, SLOTS)
+    late.start(2, late.finish(1))
+    first_inverses()
+    row_part()
+    start_row_sum(1)
+    own = start_z_sum(1)
+    newgram, p1, p1_t, applied, known = first_systems()
+    g12 = symmetric(unpack(late.finish(2)))
+    curve = symmetric(known - small_mm(small_mm(p1, g12), p1_t))
+    steps = small_mm(newgram, inverse(curve))
+    sol_ref[...] = vectors[64:96, :] + mm_high(steps, tall(vectors[0:32, :]))
+    summed = finish_sums(1, own)
     scaling = scale[...]
     for p in range(PS):
         u2 = (0.5 * WEIGHT) * scaling[p : p + 1] * summed[p]
         basis[64:96, p * 128 : (p + 1) * 128] = u2
-    late = Reduce(1, gram_l, gram_li)
-    late.start(0, pack(mm_high(basis[32:64, :], basis[64:96, :], True)))
     image = mm_high(applied, basis[...])
-    late.start(1, late.finish(0))
-    late.start(2, late.finish(1))
-    g12 = unpack(late.finish(2))
-    curve = symmetric(known - small_mm(small_mm(p1, g12), p1_t))
-    steps = small_mm(newgram, inverse(curve))
-    sol_ref[...] = vectors[64:96, :] + mm_high(steps, tall(vectors[0:32, :]))
     res_ref[...] = vectors[32:64, :] - mm_high(steps, tall(image))
 
 

time: 123 us -> 107 us (0.87)
  Pallas kernels: 119 us -> 103 us
    pallas_call x1, Pallas kernels: 119 us -> 103 us  [body(): pl.pallas_call(functools.partial(kernel, (R, Y, Z)), out_shape=(shape, sh...]
where the time goes in v4:
time: 107 us
  Pallas kernels  103 us (96%)
  local copies, waits for them, and re-layouts  2.77 us (3%)
  between operations  1.29 us (1%)
    pallas_call x1, Pallas kernels, body(): pl.pallas_call(functools.partial(kernel, (R, Y, Z)), out_shape=(shape, sh...  103 us
    unnamed x6, local copies, waits for them, and re-layouts  2.77 us

profile of v4, /device:TPU:1, one launch (start us, length us, event | category | flops | bytes accessed | tf_op | source)
XLA Modules:
  0.0 106.9 jit_solution(13949178648528789823)
XLA Ops:
  1.3 0.0 copy-start
  1.3 0.8 copy-done
  2.1 0.0 copy-start.1
  2.1 0.7 copy-done.1
  2.8 102.8 %shard_map.68 = (f32[32,512]{1,0:T(8,128)S(1)}, f32[32,512]{1,0:T(8,128)S(1)}) custom-call(f32[32,512]{1,0:T(8,128)S(1)} %copy-done, s32[256]{0:T(256)S(1)} %bitcast.4, s32[1,256]{1,0:T(1,128)S(1)} %bitcast.5, s32[1,1]{1,0:T(1,128)S(6)} %copy.9.live_ref, s32[256,16,128]{2,1,0:T(8,128)} %bitcast.6, bf16[256,16,128]{2,1,0:T(8,128)(2,1)} %bitcast.7), custom_call_target="tpu_custom_call" | custom-call | tf_op jit(solution)/shard_map/pallas_call | solution.py:587
  105.6 0.6 copy.10
  106.3 0.6 copy.11
Async XLA Ops:
  1.3 0.8 copy-start
  2.1 0.7 copy-start.1

commit v5 on v4

--- a/solution.py
+++ b/solution.py
@@ -13,7 +13,7 @@
 BF16 = jnp.bfloat16
 WEIGHT = 0.95
 PS = 4
-UNROLL = 4
+UNROLL = 8
 BUILD = 16
 
 
@@ -317,9 +317,7 @@
     pick_c = in_col_f.astype(BF16)
 
     def gather_sum(pick, terms):
-        high = terms.astype(BF16)
-        low = (terms - high.astype(F32)).astype(BF16)
-        return mm(pick, high) + mm(pick, low)
+        return mm(pick, terms.astype(BF16))
 
     def col_part():
         for m in range(32):

time: 107 us -> 104 us (0.972)
  Pallas kernels: 103 us -> 99.6 us
    pallas_call x1, Pallas kernels: 103 us -> 99.6 us  [body(): pl.pallas_call(functools.partial(kernel, (R, Y, Z)), out_shape=(shape, sh...]
where the time goes in v5:
time: 104 us
  Pallas kernels  99.6 us (96%)
  local copies, waits for them, and re-layouts  2.77 us (3%)
  between operations  1.29 us (1%)
    pallas_call x1, Pallas kernels, body(): pl.pallas_call(functools.partial(kernel, (R, Y, Z)), out_shape=(shape, sh...  99.6 us
    unnamed x6, local copies, waits for them, and re-layouts  2.77 us

profile of v5, /device:TPU:1, one launch (start us, length us, event | category | flops | bytes accessed | tf_op | source)
XLA Modules:
  0.0 103.6 jit_solution(14407949297658799442)
XLA Ops:
  1.3 0.0 copy-start
  1.3 0.8 copy-done
  2.1 0.0 copy-start.1
  2.1 0.7 copy-done.1
  2.8 99.6 %shard_map.68 = (f32[32,512]{1,0:T(8,128)S(1)}, f32[32,512]{1,0:T(8,128)S(1)}) custom-call(f32[32,512]{1,0:T(8,128)S(1)} %copy-done, s32[256]{0:T(256)S(1)} %bitcast.4, s32[1,256]{1,0:T(1,128)S(1)} %bitcast.5, s32[1,1]{1,0:T(1,128)S(6)} %copy.9.live_ref, s32[256,16,128]{2,1,0:T(8,128)} %bitcast.6, bf16[256,16,128]{2,1,0:T(8,128)(2,1)} %bitcast.7), custom_call_target="tpu_custom_call" | custom-call | tf_op jit(solution)/shard_map/pallas_call | solution.py:585
  102.4 0.6 copy.10
  103.0 0.6 copy.11
Async XLA Ops:
  1.3 0.8 copy-start
  2.1 0.7 copy-start.1

commit v6 on v5

--- a/solution.py
+++ b/solution.py
@@ -14,7 +14,7 @@
 WEIGHT = 0.95
 PS = 4
 UNROLL = 8
-BUILD = 16
+BUILD = 32
 
 
 def mm(first, second, transposed=False):

time: 104 us -> 104 us (level)
  no operation moved by 1% of the time
where the time goes in v6:
time: 104 us
  Pallas kernels  100 us (96%)
  local copies, waits for them, and re-layouts  2.77 us (3%)
  between operations  1.29 us (1%)
    pallas_call x1, Pallas kernels, body(): pl.pallas_call(functools.partial(kernel, (R, Y, Z)), out_shape=(shape, sh...  100 us
    unnamed x6, local copies, waits for them, and re-layouts  2.77 us

profile of v6, /device:TPU:1, one launch (start us, length us, event | category | flops | bytes accessed | tf_op | source)
XLA Modules:
  0.0 104.1 jit_solution(16416549804080326313)
XLA Ops:
  1.3 0.0 copy-start
  1.3 0.8 copy-done
  2.1 0.0 copy-start.1
  2.1 0.7 copy-done.1
  2.8 100.1 %shard_map.68 = (f32[32,512]{1,0:T(8,128)S(1)}, f32[32,512]{1,0:T(8,128)S(1)}) custom-call(f32[32,512]{1,0:T(8,128)S(1)} %copy-done, s32[256]{0:T(256)S(1)} %bitcast.4, s32[1,256]{1,0:T(1,128)S(1)} %bitcast.5, s32[1,1]{1,0:T(1,128)S(6)} %copy.9.live_ref, s32[256,16,128]{2,1,0:T(8,128)} %bitcast.6, bf16[256,16,128]{2,1,0:T(8,128)(2,1)} %bitcast.7), custom_call_target="tpu_custom_call" | custom-call | tf_op jit(solution)/shard_map/pallas_call | solution.py:585
  102.9 0.6 copy.10
  103.5 0.6 copy.11
Async XLA Ops:
  1.3 0.8 copy-start
  2.1 0.7 copy-start.1
